TPU v7x, 128 devices: a whole 4x4x4 slice. The times are simulated.
128 devices in a mesh: rows: 32 (over x, z_lo, y), seq: 4 (over z_hi, core).
Axes of the slice: x: 4, y: 4, z: 4 (z_hi: 2, z_lo: 2; z = z_hi * 2 + z_lo), core: 2. Of those that a mesh axis runs over, the one named last changes fastest.
Arguments:
- text_in: bfloat16 [96, 128, 768], P('rows', 'seq'), may hold values from -6 to 6
- image_in: bfloat16 [96, 144, 1024], P('rows', 'seq'), may hold values from -6 to 6
- text_lengths: int32 [96, 4], P('rows'), may hold values from 1 to 100, 128 in all within a row
- image_lengths: int32 [96, 4], P('rows'), may hold values from 1 to 112, 144 in all within a row
- text_cotangent: bfloat16 [96, 128, 768], P('rows', 'seq'), may hold values from -6 to 6
- image_cotangent: bfloat16 [96, 144, 1024], P('rows', 'seq'), may hold values from -6 to 6
- cross_text_proj: bfloat16 [768, 3, 1024], P('rows', None, 'seq'), may hold values from -0.21875 to 0.21875
- cross_text_out: bfloat16 [768, 1024], P('rows', 'seq'), may hold values from -0.75 to 0.75
- cross_text_up: bfloat16 [768, 3072], P('rows', 'seq'), may hold values from -0.21875 to 0.21875
- cross_text_down: bfloat16 [768, 3072], P('rows', 'seq'), may hold values from -0.109375 to 0.109375
- cross_text_head_bias: bfloat16 [2, 1024], P(None, 'seq'), may hold values from -1 to 1
- cross_text_up_bias: bfloat16 [1, 3072], P(None, 'seq'), may hold values from -1 to 1
- cross_text_bias: bfloat16 [4, 768], replicated, may hold values from -1 to 1
- cross_text_gain: bfloat16 [2, 768], replicated, may hold values from 0.5 to 1.5
- cross_image_proj: bfloat16 [1024, 3, 1024], P('rows', None, 'seq'), may hold values from -0.1875 to 0.1875
- cross_image_out: bfloat16 [1024, 1024], P('rows', 'seq'), may hold values from -0.75 to 0.75
- cross_image_up: bfloat16 [1024, 1024], P('rows', 'seq'), may hold values from -0.1875 to 0.1875
- cross_image_down: bfloat16 [1024, 1024], P('rows', 'seq'), may hold values from -0.1875 to 0.1875
- cross_image_head_bias: bfloat16 [2, 1024], P(None, 'seq'), may hold values from -1 to 1
- cross_image_up_bias: bfloat16 [1, 1024], P(None, 'seq'), may hold values from -1 to 1
- cross_image_bias: bfloat16 [4, 1024], replicated, may hold values from -1 to 1
- cross_image_gain: bfloat16 [2, 1024], replicated, may hold values from 0.5 to 1.5
- self_text_proj: bfloat16 [768, 3, 768], P('rows', None, 'seq'), may hold values from -0.21875 to 0.21875
- self_text_out: bfloat16 [768, 768], P('rows', 'seq'), may hold values from -0.875 to 0.875
- self_text_up: bfloat16 [768, 3072], P('rows', 'seq'), may hold values from -0.21875 to 0.21875
- self_text_down: bfloat16 [768, 3072], P('rows', 'seq'), may hold values from -0.109375 to 0.109375
- self_text_head_bias: bfloat16 [2, 768], P(None, 'seq'), may hold values from -1 to 1
- self_text_up_bias: bfloat16 [1, 3072], P(None, 'seq'), may hold values from -1 to 1
- self_text_bias: bfloat16 [4, 768], replicated, may hold values from -1 to 1
- self_text_gain: bfloat16 [2, 768], replicated, may hold values from 0.5 to 1.5
- self_image_proj: bfloat16 [1024, 3, 1024], P('rows', None, 'seq'), may hold values from -0.1875 to 0.1875
- self_image_out: bfloat16 [1024, 1024], P('rows', 'seq'), may hold values from -0.75 to 0.75
- self_image_up: bfloat16 [1024, 1024], P('rows', 'seq'), may hold values from -0.1875 to 0.1875
- self_image_down: bfloat16 [1024, 1024], P('rows', 'seq'), may hold values from -0.1875 to 0.1875
- self_image_head_bias: bfloat16 [2, 1024], P(None, 'seq'), may hold values from -1 to 1
- self_image_up_bias: bfloat16 [1, 1024], P(None, 'seq'), may hold values from -1 to 1
- self_image_bias: bfloat16 [4, 1024], replicated, may hold values from -1 to 1
- self_image_gain: bfloat16 [2, 1024], replicated, may hold values from 0.5 to 1.5
Outputs:
- text_out: bfloat16 [96, 128, 768], P('rows', 'seq')
- image_out: bfloat16 [96, 144, 1024], P('rows', 'seq')
- text_grad: bfloat16 [96, 128, 768], P('rows', 'seq')
- image_grad: bfloat16 [96, 144, 1024], P('rows', 'seq')
- grad_cross_text_proj: float32 [768, 3, 1024], P('rows', None, 'seq')
- grad_cross_text_out: float32 [768, 1024], P('rows', 'seq')
- grad_cross_text_up: float32 [768, 3072], P('rows', 'seq')
- grad_cross_text_down: float32 [768, 3072], P('rows', 'seq')
- grad_cross_text_head_bias: float32 [2, 1024], P(None, 'seq')
- grad_cross_text_up_bias: float32 [1, 3072], P(None, 'seq')
- grad_cross_text_bias: float32 [4, 768], replicated
- grad_cross_text_gain: float32 [2, 768], replicated
- grad_cross_image_proj: float32 [1024, 3, 1024], P('rows', None, 'seq')
- grad_cross_image_out: float32 [1024, 1024], P('rows', 'seq')
- grad_cross_image_up: float32 [1024, 1024], P('rows', 'seq')
- grad_cross_image_down: float32 [1024, 1024], P('rows', 'seq')
- grad_cross_image_head_bias: float32 [2, 1024], P(None, 'seq')
- grad_cross_image_up_bias: float32 [1, 1024], P(None, 'seq')
- grad_cross_image_bias: float32 [4, 1024], replicated
- grad_cross_image_gain: float32 [2, 1024], replicated
- grad_self_text_proj: float32 [768, 3, 768], P('rows', None, 'seq')
- grad_self_text_out: float32 [768, 768], P('rows', 'seq')
- grad_self_text_up: float32 [768, 3072], P('rows', 'seq')
- grad_self_text_down: float32 [768, 3072], P('rows', 'seq')
- grad_self_text_head_bias: float32 [2, 768], P(None, 'seq')
- grad_self_text_up_bias: float32 [1, 3072], P(None, 'seq')
- grad_self_text_bias: float32 [4, 768], replicated
- grad_self_text_gain: float32 [2, 768], replicated
- grad_self_image_proj: float32 [1024, 3, 1024], P('rows', None, 'seq')
- grad_self_image_out: float32 [1024, 1024], P('rows', 'seq')
- grad_self_image_up: float32 [1024, 1024], P('rows', 'seq')
- grad_self_image_down: float32 [1024, 1024], P('rows', 'seq')
- grad_self_image_head_bias: float32 [2, 1024], P(None, 'seq')
- grad_self_image_up_bias: float32 [1, 1024], P(None, 'seq')
- grad_self_image_bias: float32 [4, 1024], replicated
- grad_self_image_gain: float32 [2, 1024], replicated
Inputs may be any that keep to these rules, and one draw needn't show every extreme that they name: `text_lengths`: each row's 4 caption lengths sum to 128, and one of them is exactly 100. `image_lengths`: each row's 4 image lengths sum to 144, and one of them is exactly 112.
All inputs are finite; a program needn't handle non-finite values.
Results may differ from a plain program's by a relative error of at most 0.038.
Values may be sent and summed in bfloat16 or wider, within the bound.
A program may use at most 128 MiB of HBM per device.

v0:
```python
import jax
import jax.numpy as jnp
from jax import lax
from jax.sharding import PartitionSpec as P

DT = 768
DI = 1024
DC = 1024
HEADS_CROSS = 8
HEADS_TEXT = 12
HEADS_IMAGE = 8


epsilon = 1e-05
masked_value = -1000000000.0


def segments(lengths, positions_total):
    boundary = jnp.cumsum(lengths, axis=-1)
    position = jnp.arange(positions_total, dtype=jnp.int32)
    return jnp.sum((position[None, :, None] >= boundary[:, None, :]).astype(jnp.int32), axis=-1)


def layer_norm(summed, gain_vec, shift_vec):
    centre = jnp.mean(summed, axis=-1, keepdims=True)
    spread = jnp.mean(jnp.square(summed - centre), axis=-1, keepdims=True)
    return (summed - centre) * lax.rsqrt(spread + epsilon) * gain_vec + shift_vec


def spread_tokens(text_part, image_part):
    return (
        lax.all_gather(text_part, "seq", axis=1, tiled=True),
        lax.all_gather(image_part, "seq", axis=1, tiled=True),
    )


def tokens_from_partials(text_part, image_part):
    return (
        lax.psum_scatter(
            text_part.astype(jnp.bfloat16), "seq", scatter_dimension=1, tiled=True
        ).astype(jnp.float32),
        lax.psum_scatter(
            image_part.astype(jnp.bfloat16), "seq", scatter_dimension=1, tiled=True
        ).astype(jnp.float32),
    )


def spread_gradients(text_part, image_part):
    return (
        lax.all_gather(text_part, "seq", axis=1, tiled=True),
        lax.all_gather(image_part, "seq", axis=1, tiled=True),
    )


def gradients_from_partials(text_part, image_part):
    return (
        lax.psum_scatter(
            text_part.astype(jnp.bfloat16), "seq", scatter_dimension=1, tiled=True
        ).astype(jnp.float32),
        lax.psum_scatter(
            image_part.astype(jnp.bfloat16), "seq", scatter_dimension=1, tiled=True
        ).astype(jnp.float32),
    )


def heads_of(values_flat, head_size):
    return values_flat.reshape(
        values_flat.shape[0], values_flat.shape[1], values_flat.shape[2] // head_size, head_size
    )


def project_local(inputs_low, weights):
    head_bias = weights[4].astype(jnp.float32)
    offset = jnp.stack([head_bias[0], jnp.zeros_like(head_bias[0]), head_bias[1]])
    result = (
        jnp.einsum("rtd,dca->rtca", inputs_low, weights[0], preferred_element_type=jnp.float32)
        + offset
    )
    return result.astype(jnp.bfloat16)


def stream_sources(projected, crossing):
    partner = [1, 0] if crossing else [0, 1]
    sources = []
    for stream in range(2):
        key_source = projected[partner[stream]]
        sources.append((projected[stream][:, :, 0], key_source[:, :, 1], key_source[:, :, 2]))
    return sources


def attend_local(queries, keys_in, values_in, allowed, head_size):
    query_heads = heads_of(queries, head_size)
    key_heads = heads_of(keys_in, head_size)
    value_heads = heads_of(values_in, head_size)
    scaling = head_size ** (-0.5)
    raw_scores = jnp.einsum(
        "bqhd,bkhd->bhqk", query_heads, key_heads, preferred_element_type=jnp.float32
    )
    scores = jnp.where(allowed[:, None], raw_scores * scaling, masked_value)
    largest = jnp.max(scores, axis=-1, keepdims=True)
    shifted = jnp.exp(scores - largest)
    total_mass = jnp.sum(shifted, axis=-1, keepdims=True)
    probability = (shifted / total_mass).astype(jnp.bfloat16)
    mixed = jnp.einsum(
        "bhqk,bkhd->bqhd", probability, value_heads, preferred_element_type=jnp.float32
    )
    return (mixed.reshape(queries.shape).astype(jnp.bfloat16), largest + jnp.log(total_mass))


def attend_back(queries, keys_in, values_in, allowed, logsum, grad_mixed, head_size):
    query_heads = heads_of(queries, head_size)
    key_heads = heads_of(keys_in, head_size)
    value_heads = heads_of(values_in, head_size)
    scaling = head_size ** (-0.5)
    raw_scores = jnp.einsum(
        "bqhd,bkhd->bhqk", query_heads, key_heads, preferred_element_type=jnp.float32
    )
    scores = jnp.where(allowed[:, None], raw_scores * scaling, masked_value)
    probability = jnp.exp(scores - logsum)
    grad_heads = heads_of(grad_mixed, head_size)
    grad_prob = jnp.einsum(
        "bqhd,bkhd->bhqk", grad_heads, value_heads, preferred_element_type=jnp.float32
    )
    grad_values = jnp.einsum(
        "bhqk,bqhd->bkhd",
        probability.astype(jnp.bfloat16),
        grad_heads,
        preferred_element_type=jnp.float32,
    )
    row_inner = jnp.sum(grad_prob * probability, axis=-1, keepdims=True)
    grad_scores = (probability * (grad_prob - row_inner) * scaling).astype(jnp.bfloat16)
    grad_queries = jnp.einsum(
        "bhqk,bkhd->bqhd", grad_scores, key_heads, preferred_element_type=jnp.float32
    )
    grad_keys = jnp.einsum(
        "bhqk,bqhd->bkhd", grad_scores, query_heads, preferred_element_type=jnp.float32
    )
    return (
        grad_queries.reshape(queries.shape).astype(jnp.bfloat16),
        grad_keys.reshape(keys_in.shape).astype(jnp.bfloat16),
        grad_values.reshape(values_in.shape).astype(jnp.bfloat16),
    )


def mlp_forward(normed_low, up_weight, down_weight, up_bias):
    upward = jnp.einsum(
        "rtd,df->rtf", normed_low, up_weight, preferred_element_type=jnp.float32
    ) + up_bias[0].astype(jnp.float32)
    active = jax.nn.gelu(upward).astype(jnp.bfloat16)
    partial_sum = jnp.einsum("rtf,df->rtd", active, down_weight, preferred_element_type=jnp.float32)
    return (upward, active, partial_sum)


def mlp_backward(grad_low, normed_low, upward, active, up_weight, down_weight):
    grad_down = jnp.einsum("rtd,rtf->df", grad_low, active, preferred_element_type=jnp.float32)
    grad_active = jnp.einsum(
        "rtd,df->rtf", grad_low, down_weight, preferred_element_type=jnp.float32
    )
    unused, gelu_pullback = jax.vjp(jax.nn.gelu, upward)
    grad_upward = gelu_pullback(grad_active)[0].astype(jnp.bfloat16)
    grad_up = jnp.einsum("rtd,rtf->df", normed_low, grad_upward, preferred_element_type=jnp.float32)
    up_bias_grad = jnp.sum(grad_upward, axis=(0, 1), dtype=jnp.float32)[None]
    partial_sum = jnp.einsum(
        "rtf,df->rtd", grad_upward, up_weight, preferred_element_type=jnp.float32
    )
    return (grad_up, grad_down, up_bias_grad, partial_sum)


def forward_block(inputs, weights, mask_pair, head_sizes, crossing):
    lowered = spread_tokens(inputs[0].astype(jnp.bfloat16), inputs[1].astype(jnp.bfloat16))
    projected = [project_local(lowered[stream], weights[stream]) for stream in range(2)]
    sources = stream_sources(projected, crossing)
    attended = [
        attend_local(
            sources[stream][0],
            sources[stream][1],
            sources[stream][2],
            mask_pair[stream],
            head_sizes[stream],
        )
        for stream in range(2)
    ]
    partials = [
        jnp.einsum(
            "rta,da->rtd",
            attended[stream][0],
            weights[stream][1],
            preferred_element_type=jnp.float32,
        )
        for stream in range(2)
    ]
    summed = tokens_from_partials(partials[0], partials[1])
    first_sums = []
    normed_rows = []
    for stream in range(2):
        bias_rows = weights[stream][6].astype(jnp.float32)
        gain_rows = weights[stream][7].astype(jnp.float32)
        first_sum = inputs[stream] + summed[stream] + bias_rows[0]
        first_sums.append(first_sum)
        normed_rows.append(layer_norm(first_sum, gain_rows[0], bias_rows[2]))
    normed_low = [normed_rows[stream].astype(jnp.bfloat16) for stream in range(2)]
    widened = spread_tokens(normed_low[0], normed_low[1])
    feeding = [(weights[stream][2], weights[stream][3], weights[stream][5]) for stream in range(2)]
    lifted = [
        mlp_forward(widened[stream], feeding[stream][0], feeding[stream][1], feeding[stream][2])
        for stream in range(2)
    ]
    down_sums = tokens_from_partials(lifted[0][2], lifted[1][2])
    results = []
    stored = []
    for stream in range(2):
        bias_rows = weights[stream][6].astype(jnp.float32)
        gain_rows = weights[stream][7].astype(jnp.float32)
        second_sum = normed_rows[stream] + down_sums[stream] + bias_rows[1]
        results.append(layer_norm(second_sum, gain_rows[1], bias_rows[3]))
        stored.append(
            (
                lowered[stream],
                projected[stream],
                attended[stream][1],
                attended[stream][0],
                first_sums[stream],
                widened[stream],
                lifted[stream][0],
                lifted[stream][1],
                second_sum,
                feeding[stream],
            )
        )
    return (results, stored)


def backward_block(incoming, stored, weights, mask_pair, head_sizes, crossing):
    grad_seconds = []
    second_lows = []
    down_bias_grads = []
    second_gain_grads = []
    second_shift_grads = []
    for stream in range(2):
        bias_rows = weights[stream][6].astype(jnp.float32)
        gain_rows = weights[stream][7].astype(jnp.float32)
        unused, norm_pullback = jax.vjp(layer_norm, stored[stream][8], gain_rows[1], bias_rows[3])
        grad_second, gain_grad, shift_grad = norm_pullback(incoming[stream])
        second_low = grad_second.astype(jnp.bfloat16)
        grad_seconds.append(grad_second)
        second_lows.append(second_low)
        down_bias_grads.append(jnp.sum(second_low, axis=(0, 1), dtype=jnp.float32))
        second_gain_grads.append(gain_grad)
        second_shift_grads.append(shift_grad)
    widened = spread_gradients(second_lows[0], second_lows[1])
    backed = [
        mlp_backward(
            widened[stream],
            stored[stream][5],
            stored[stream][6],
            stored[stream][7],
            stored[stream][9][0],
            stored[stream][9][1],
        )
        for stream in range(2)
    ]
    returned = gradients_from_partials(backed[0][3], backed[1][3])
    mlp_totals = [(backed[stream][0], backed[stream][1], backed[stream][2]) for stream in range(2)]
    grad_firsts = []
    first_lows = []
    out_bias_grads = []
    first_gain_grads = []
    first_shift_grads = []
    for stream in range(2):
        bias_rows = weights[stream][6].astype(jnp.float32)
        gain_rows = weights[stream][7].astype(jnp.float32)
        grad_normed = grad_seconds[stream] + returned[stream]
        unused, norm_pullback = jax.vjp(layer_norm, stored[stream][4], gain_rows[0], bias_rows[2])
        grad_first, gain_grad, shift_grad = norm_pullback(grad_normed)
        first_low = grad_first.astype(jnp.bfloat16)
        grad_firsts.append(grad_first)
        first_lows.append(first_low)
        out_bias_grads.append(jnp.sum(first_low, axis=(0, 1), dtype=jnp.float32))
        first_gain_grads.append(gain_grad)
        first_shift_grads.append(shift_grad)
    branch_wide = spread_gradients(first_lows[0], first_lows[1])
    out_grads = [
        jnp.einsum(
            "rtd,rta->da",
            branch_wide[stream],
            stored[stream][3],
            preferred_element_type=jnp.float32,
        )
        for stream in range(2)
    ]
    mixed_grads = [
        jnp.einsum(
            "rtd,da->rta",
            branch_wide[stream],
            weights[stream][1],
            preferred_element_type=jnp.float32,
        ).astype(jnp.bfloat16)
        for stream in range(2)
    ]
    sources = stream_sources([stored[0][1], stored[1][1]], crossing)
    attention_back = [
        attend_back(
            sources[stream][0],
            sources[stream][1],
            sources[stream][2],
            mask_pair[stream],
            stored[stream][2],
            mixed_grads[stream],
            head_sizes[stream],
        )
        for stream in range(2)
    ]
    partner = [1, 0] if crossing else [0, 1]
    proj_grads = [
        jnp.stack(
            (
                attention_back[stream][0],
                attention_back[partner[stream]][1],
                attention_back[partner[stream]][2],
            ),
            axis=2,
        )
        for stream in range(2)
    ]
    input_partials = [
        jnp.einsum(
            "rtca,dca->rtd",
            proj_grads[stream],
            weights[stream][0],
            preferred_element_type=jnp.float32,
        )
        for stream in range(2)
    ]
    input_returned = gradients_from_partials(input_partials[0], input_partials[1])
    next_grads = []
    matrices = []
    columns = []
    vectors = []
    for stream in range(2):
        next_grads.append(grad_firsts[stream] + input_returned[stream])
        proj_weight_grad = jnp.einsum(
            "rtd,rtca->dca",
            stored[stream][0],
            proj_grads[stream],
            preferred_element_type=jnp.float32,
        )
        head_bias_grad = jnp.stack(
            [
                jnp.sum(proj_grads[stream][:, :, 0], axis=(0, 1), dtype=jnp.float32),
                jnp.sum(proj_grads[stream][:, :, 2], axis=(0, 1), dtype=jnp.float32),
            ]
        )
        matrices.append(
            (proj_weight_grad, out_grads[stream], mlp_totals[stream][0], mlp_totals[stream][1])
        )
        columns.append((head_bias_grad, mlp_totals[stream][2]))
        vectors.append(
            (
                jnp.stack(
                    [
                        out_bias_grads[stream],
                        down_bias_grads[stream],
                        first_shift_grads[stream],
                        second_shift_grads[stream],
                    ]
                ),
                jnp.stack([first_gain_grads[stream], second_gain_grads[stream]]),
            )
        )
    return (next_grads, matrices, columns, vectors)


def on_device(
    text_in,
    image_in,
    text_lengths,
    image_lengths,
    text_cotangent,
    image_cotangent,
    cross_text_proj,
    cross_text_out,
    cross_text_up,
    cross_text_down,
    cross_text_head_bias,
    cross_text_up_bias,
    cross_text_bias,
    cross_text_gain,
    cross_image_proj,
    cross_image_out,
    cross_image_up,
    cross_image_down,
    cross_image_head_bias,
    cross_image_up_bias,
    cross_image_bias,
    cross_image_gain,
    self_text_proj,
    self_text_out,
    self_text_up,
    self_text_down,
    self_text_head_bias,
    self_text_up_bias,
    self_text_bias,
    self_text_gain,
    self_image_proj,
    self_image_out,
    self_image_up,
    self_image_down,
    self_image_head_bias,
    self_image_up_bias,
    self_image_bias,
    self_image_gain,
):
    seq_count = lax.axis_size("seq")
    text_seg = segments(text_lengths, text_in.shape[1] * seq_count)
    image_seg = segments(image_lengths, image_in.shape[1] * seq_count)
    cross_masks = (
        text_seg[:, :, None] == image_seg[:, None, :],
        image_seg[:, :, None] == text_seg[:, None, :],
    )
    own_masks = (
        text_seg[:, :, None] == text_seg[:, None, :],
        image_seg[:, :, None] == image_seg[:, None, :],
    )
    cross_heads = (DC // HEADS_CROSS, DC // HEADS_CROSS)
    self_heads = (DT // HEADS_TEXT, DI // HEADS_IMAGE)
    cross_fetched = (
        lax.all_gather(cross_text_proj, "rows", axis=0, tiled=True),
        lax.all_gather(cross_text_out, "rows", axis=0, tiled=True),
        lax.all_gather(cross_text_up, "rows", axis=0, tiled=True),
        lax.all_gather(cross_text_down, "rows", axis=0, tiled=True),
        lax.all_gather(cross_image_proj, "rows", axis=0, tiled=True),
        lax.all_gather(cross_image_out, "rows", axis=0, tiled=True),
        lax.all_gather(cross_image_up, "rows", axis=0, tiled=True),
        lax.all_gather(cross_image_down, "rows", axis=0, tiled=True),
    )
    cross_blocks = [
        (
            cross_fetched[0],
            cross_fetched[1],
            cross_fetched[2],
            cross_fetched[3],
            cross_text_head_bias,
            cross_text_up_bias,
            cross_text_bias,
            cross_text_gain,
        ),
        (
            cross_fetched[4],
            cross_fetched[5],
            cross_fetched[6],
            cross_fetched[7],
            cross_image_head_bias,
            cross_image_up_bias,
            cross_image_bias,
            cross_image_gain,
        ),
    ]
    middle, cross_stored = forward_block(
        (text_in.astype(jnp.float32), image_in.astype(jnp.float32)),
        cross_blocks,
        cross_masks,
        cross_heads,
        True,
    )
    self_fetched = (
        lax.all_gather(self_text_proj, "rows", axis=0, tiled=True),
        lax.all_gather(self_text_out, "rows", axis=0, tiled=True),
        lax.all_gather(self_text_up, "rows", axis=0, tiled=True),
        lax.all_gather(self_text_down, "rows", axis=0, tiled=True),
        lax.all_gather(self_image_proj, "rows", axis=0, tiled=True),
        lax.all_gather(self_image_out, "rows", axis=0, tiled=True),
        lax.all_gather(self_image_up, "rows", axis=0, tiled=True),
        lax.all_gather(self_image_down, "rows", axis=0, tiled=True),
    )
    self_blocks = [
        (
            self_fetched[0],
            self_fetched[1],
            self_fetched[2],
            self_fetched[3],
            self_text_head_bias,
            self_text_up_bias,
            self_text_bias,
            self_text_gain,
        ),
        (
            self_fetched[4],
            self_fetched[5],
            self_fetched[6],
            self_fetched[7],
            self_image_head_bias,
            self_image_up_bias,
            self_image_bias,
            self_image_gain,
        ),
    ]
    final, self_stored = forward_block(
        (middle[0], middle[1]), self_blocks, own_masks, self_heads, False
    )
    self_back = backward_block(
        (text_cotangent.astype(jnp.float32), image_cotangent.astype(jnp.float32)),
        self_stored,
        self_blocks,
        own_masks,
        self_heads,
        False,
    )
    self_mats = self_back[1]
    self_sums = (
        lax.psum_scatter(
            self_mats[0][0].astype(jnp.bfloat16), "rows", scatter_dimension=0, tiled=True
        ).astype(jnp.float32),
        lax.psum_scatter(
            self_mats[0][1].astype(jnp.bfloat16), "rows", scatter_dimension=0, tiled=True
        ).astype(jnp.float32),
        lax.psum_scatter(
            self_mats[0][2].astype(jnp.bfloat16), "rows", scatter_dimension=0, tiled=True
        ).astype(jnp.float32),
        lax.psum_scatter(
            self_mats[0][3].astype(jnp.bfloat16), "rows", scatter_dimension=0, tiled=True
        ).astype(jnp.float32),
        lax.psum_scatter(
            self_mats[1][0].astype(jnp.bfloat16), "rows", scatter_dimension=0, tiled=True
        ).astype(jnp.float32),
        lax.psum_scatter(
            self_mats[1][1].astype(jnp.bfloat16), "rows", scatter_dimension=0, tiled=True
        ).astype(jnp.float32),
        lax.psum_scatter(
            self_mats[1][2].astype(jnp.bfloat16), "rows", scatter_dimension=0, tiled=True
        ).astype(jnp.float32),
        lax.psum_scatter(
            self_mats[1][3].astype(jnp.bfloat16), "rows", scatter_dimension=0, tiled=True
        ).astype(jnp.float32),
    )
    cross_back = backward_block(
        (self_back[0][0], self_back[0][1]),
        cross_stored,
        cross_blocks,
        cross_masks,
        cross_heads,
        True,
    )
    cross_mats = cross_back[1]
    cross_sums = (
        lax.psum_scatter(
            cross_mats[0][0].astype(jnp.bfloat16), "rows", scatter_dimension=0, tiled=True
        ).astype(jnp.float32),
        lax.psum_scatter(
            cross_mats[0][1].astype(jnp.bfloat16), "rows", scatter_dimension=0, tiled=True
        ).astype(jnp.float32),
        lax.psum_scatter(
            cross_mats[0][2].astype(jnp.bfloat16), "rows", scatter_dimension=0, tiled=True
        ).astype(jnp.float32),
        lax.psum_scatter(
            cross_mats[0][3].astype(jnp.bfloat16), "rows", scatter_dimension=0, tiled=True
        ).astype(jnp.float32),
        lax.psum_scatter(
            cross_mats[1][0].astype(jnp.bfloat16), "rows", scatter_dimension=0, tiled=True
        ).astype(jnp.float32),
        lax.psum_scatter(
            cross_mats[1][1].astype(jnp.bfloat16), "rows", scatter_dimension=0, tiled=True
        ).astype(jnp.float32),
        lax.psum_scatter(
            cross_mats[1][2].astype(jnp.bfloat16), "rows", scatter_dimension=0, tiled=True
        ).astype(jnp.float32),
        lax.psum_scatter(
            cross_mats[1][3].astype(jnp.bfloat16), "rows", scatter_dimension=0, tiled=True
        ).astype(jnp.float32),
    )
    cross_cols = cross_back[2]
    self_cols = self_back[2]
    column_totals = lax.psum(
        (
            cross_cols[0][0],
            cross_cols[0][1],
            cross_cols[1][0],
            cross_cols[1][1],
            self_cols[0][0],
            self_cols[0][1],
            self_cols[1][0],
            self_cols[1][1],
        ),
        "rows",
    )
    cross_vecs = cross_back[3]
    self_vecs = self_back[3]
    vector_totals = lax.psum(
        (
            cross_vecs[0][0],
            cross_vecs[0][1],
            cross_vecs[1][0],
            cross_vecs[1][1],
            self_vecs[0][0],
            self_vecs[0][1],
            self_vecs[1][0],
            self_vecs[1][1],
        ),
        ("rows", "seq"),
    )
    text_grad = cross_back[0][0].astype(jnp.bfloat16)
    image_grad = cross_back[0][1].astype(jnp.bfloat16)
    return (
        final[0].astype(jnp.bfloat16),
        final[1].astype(jnp.bfloat16),
        text_grad,
        image_grad,
        cross_sums[0],
        cross_sums[1],
        cross_sums[2],
        cross_sums[3],
        column_totals[0],
        column_totals[1],
        vector_totals[0],
        vector_totals[1],
        cross_sums[4],
        cross_sums[5],
        cross_sums[6],
        cross_sums[7],
        column_totals[2],
        column_totals[3],
        vector_totals[2],
        vector_totals[3],
        self_sums[0],
        self_sums[1],
        self_sums[2],
        self_sums[3],
        column_totals[4],
        column_totals[5],
        vector_totals[4],
        vector_totals[5],
        self_sums[4],
        self_sums[5],
        self_sums[6],
        self_sums[7],
        column_totals[6],
        column_totals[7],
        vector_totals[6],
        vector_totals[7],
    )


def solution(mesh):
    placed = (
        P("rows", "seq", None),
        P("rows", "seq", None),
        P("rows", None),
        P("rows", None),
        P("rows", "seq", None),
        P("rows", "seq", None),
        P("rows", None, "seq"),
        P("rows", "seq"),
        P("rows", "seq"),
        P("rows", "seq"),
        P(None, "seq"),
        P(None, "seq"),
        P(),
        P(),
        P("rows", None, "seq"),
        P("rows", "seq"),
        P("rows", "seq"),
        P("rows", "seq"),
        P(None, "seq"),
        P(None, "seq"),
        P(),
        P(),
        P("rows", None, "seq"),
        P("rows", "seq"),
        P("rows", "seq"),
        P("rows", "seq"),
        P(None, "seq"),
        P(None, "seq"),
        P(),
        P(),
        P("rows", None, "seq"),
        P("rows", "seq"),
        P("rows", "seq"),
        P("rows", "seq"),
        P(None, "seq"),
        P(None, "seq"),
        P(),
        P(),
    )
    return jax.shard_map(
        on_device,
        mesh=mesh,
        in_specs=placed,
        out_specs=(
            P("rows", "seq", None),
            P("rows", "seq", None),
            P("rows", "seq", None),
            P("rows", "seq", None),
            P("rows", None, "seq"),
            P("rows", "seq"),
            P("rows", "seq"),
            P("rows", "seq"),
            P(None, "seq"),
            P(None, "seq"),
            P(),
            P(),
            P("rows", None, "seq"),
            P("rows", "seq"),
            P("rows", "seq"),
            P("rows", "seq"),
            P(None, "seq"),
            P(None, "seq"),
            P(),
            P(),
            P("rows", None, "seq"),
            P("rows", "seq"),
            P("rows", "seq"),
            P("rows", "seq"),
            P(None, "seq"),
            P(None, "seq"),
            P(),
            P(),
            P("rows", None, "seq"),
            P("rows", "seq"),
            P("rows", "seq"),
            P("rows", "seq"),
            P(None, "seq"),
            P(None, "seq"),
            P(),
            P(),
        ),
        check_vma=False,
    )
```

profile of v0, /device:TPU:1, one launch (start us, length us, event | category | flops | bytes accessed | tf_op | source)
XLA Modules:
  0.0 4423.8 jit_solution(5952630544210876339)
XLA Ops:
  24.4 71.5 %all_gather.110 = bf16[1024,256]{1,0:T(8,128)(2,1)S(1)} all-gather(bf16[32,256]{1,0:T(8,128)(2,1)S(1)} %copy-done.194), channel_id=1, replica_groups=mesh['rows'=32,'seq'=4] {'rows'}, dimensions={0}, use_global_device_ids=true | all-gather | bytes 540672 | tf_op jit(solution)/shard_map/all_gather | solution.py:432
  146.1 152.2 %all-gather.8.cloned.1.call-done = bf16[1024,3,256]{2,0,1:T(8,128)(2,1)} async-done(((bf16[32,3,256]{2,0,1:T(8,128)(2,1)}), bf16[1024,3,256]{2,0,1:T(8,128)(2,1)}) %all-gather.8.cloned.1.call-update) | async-done | bytes 1572880 | tf_op jit(solution)/shard_map/all_gather | solution.py:431
  304.3 69.1 %all_gather.100 = bf16[768,256]{1,0:T(8,128)(2,1)S(1)} all-gather(bf16[24,256]{1,0:T(8,128)(2,1)S(1)} %copy-done.207), channel_id=1, replica_groups=mesh['rows'=32,'seq'=4] {'rows'}, dimensions={0}, use_global_device_ids=true | all-gather | bytes 405504 | tf_op jit(solution)/shard_map/all_gather | solution.py:428
  378.6 64.7 %all_gather.112 = bf16[1024,256]{1,0:T(8,128)(2,1)S(1)} all-gather(bf16[32,256]{1,0:T(8,128)(2,1)S(1)} %copy-done.195), channel_id=1, replica_groups=mesh['rows'=32,'seq'=4] {'rows'}, dimensions={0}, use_global_device_ids=true | all-gather | bytes 540672 | tf_op jit(solution)/shard_map/all_gather | solution.py:433
  444.6 66.9 %all_gather.113 = bf16[1024,256]{1,0:T(8,128)(2,1)S(1)} all-gather(bf16[32,256]{1,0:T(8,128)(2,1)S(1)} %copy-done.196), channel_id=1, replica_groups=mesh['rows'=32,'seq'=4] {'rows'}, dimensions={0}, use_global_device_ids=true | all-gather | bytes 540672 | tf_op jit(solution)/shard_map/all_gather | solution.py:434
  514.6 74.6 %all_gather.111 = bf16[3,144,1024]{2,0,1:T(4,128)(2,1)S(1)} all-gather(bf16[3,36,1024]{2,0,1:T(4,128)(2,1)S(1)} %copy.270), channel_id=1, replica_groups=mesh['rows'=32,'seq'=4] {'seq'}, dimensions={1}, use_global_device_ids=true | all-gather | bytes 1105920 | tf_op jit(solution)/shard_map/all_gather | solution.py:33
  594.9 64.5 %all_gather.106 = bf16[768,192]{1,0:T(8,128)(2,1)S(1)} all-gather(bf16[24,192]{1,0:T(8,128)(2,1)S(1)} %copy-done.208), channel_id=1, replica_groups=mesh['rows'=32,'seq'=4] {'rows'}, dimensions={0}, use_global_device_ids=true | all-gather | bytes 304128 | tf_op jit(solution)/shard_map/all_gather | solution.py:467
  660.1 67.6 %all_gather.116 = bf16[1024,256]{1,0:T(8,128)(2,1)S(1)} all-gather(bf16[32,256]{1,0:T(8,128)(2,1)S(1)} %copy-done.197), channel_id=1, replica_groups=mesh['rows'=32,'seq'=4] {'rows'}, dimensions={0}, use_global_device_ids=true | all-gather | bytes 540672 | tf_op jit(solution)/shard_map/all_gather | solution.py:471
  727.8 69.6 %all_gather.118 = bf16[1024,256]{1,0:T(8,128)(2,1)} all-gather(bf16[32,256]{1,0:T(8,128)(2,1)S(1)} %copy-done.198), channel_id=1, replica_groups=mesh['rows'=32,'seq'=4] {'rows'}, dimensions={0}, use_global_device_ids=true | all-gather | bytes 540672 | tf_op jit(solution)/shard_map/all_gather | solution.py:472
  797.4 73.6 %all_gather.119 = bf16[1024,256]{1,0:T(8,128)(2,1)} all-gather(bf16[32,256]{1,0:T(8,128)(2,1)S(1)} %copy-done.199), channel_id=1, replica_groups=mesh['rows'=32,'seq'=4] {'rows'}, dimensions={0}, use_global_device_ids=true | all-gather | bytes 540672 | tf_op jit(solution)/shard_map/all_gather | solution.py:473
  870.9 78.4 %all_gather.105 = bf16[768,3,192]{2,0,1:T(8,128)(2,1)} all-gather(bf16[24,3,192]{2,0,1:T(8,128)(2,1)S(1)} %copy-done.125), channel_id=1, replica_groups=mesh['rows'=32,'seq'=4] {'rows'}, dimensions={0}, use_global_device_ids=true | all-gather | bytes 912384 | tf_op jit(solution)/shard_map/all_gather | solution.py:466
  952.5 68.5 %all_gather.101 = bf16[3,128,768]{2,1,0:T(8,128)(2,1)S(1)} all-gather(bf16[3,32,768]{2,1,0:T(8,128)(2,1)S(1)} %fusion.223), channel_id=1, replica_groups=mesh['rows'=32,'seq'=4] {'seq'}, dimensions={1}, use_global_device_ids=true | all-gather | bytes 737280 | tf_op jit(solution)/shard_map/all_gather | solution.py:32
  1122.9 37.8 all-reduce.31.cloned.1.call-done
  1219.2 103.4 %all-gather.16.cloned.1.call-done = bf16[768,768]{1,0:T(8,128)(2,1)} async-done(((bf16[24,768]{1,0:T(8,128)(2,1)}), bf16[768,768]{1,0:T(8,128)(2,1)}) %all-gather.16.cloned.1.call-update) | async-done | bytes 1179664 | tf_op jit(solution)/shard_map/all_gather | solution.py:468
  1325.7 149.6 %all-gather.18.cloned.1.call-done = bf16[768,768]{1,0:T(8,128)(2,1)} async-done(((bf16[24,768]{1,0:T(8,128)(2,1)}), bf16[768,768]{1,0:T(8,128)(2,1)}) %all-gather.18.cloned.1.call-update) | async-done | bytes 1179664 | tf_op jit(solution)/shard_map/all_gather | solution.py:469
  1478.7 65.5 %all-reduce.33.cloned.1.call-done = bf16[3,144,1024]{2,1,0:T(8,128)(2,1)} async-done(((bf16[3,144,1024]{2,1,0:T(8,128)(2,1)}), bf16[3,144,1024]{2,1,0:T(8,128)(2,1)}) %all-reduce.33.cloned.1.call-update) | async-done | bytes 884752
  1847.5 71.1 %reduce-scatter.71.cloned.1.call-done = bf16[32,256]{1,0:T(8,128)(2,1)} async-done(((bf16[1024,256]{1,0:T(8,128)(2,1)}), bf16[32,256]{1,0:T(8,128)(2,1)}) %reduce-scatter.71.cloned.1.call-update) | async-done | bytes 16400 | tf_op jit(solution)/shard_map/reduce_scatter | solution.py:531
  1920.0 157.0 %reduce-scatter.69.cloned.1.call-done = bf16[32,256]{1,0:T(8,128)(2,1)} async-done(((bf16[1024,256]{1,0:T(8,128)(2,1)}), bf16[32,256]{1,0:T(8,128)(2,1)}) %reduce-scatter.69.cloned.1.call-update) | async-done | bytes 16400 | tf_op jit(solution)/shard_map/reduce_scatter | solution.py:528
  2078.4 156.9 %reduce-scatter.67.cloned.1.call-done = bf16[32,256]{1,0:T(8,128)(2,1)} async-done(((bf16[1024,256]{1,0:T(8,128)(2,1)}), bf16[32,256]{1,0:T(8,128)(2,1)}) %reduce-scatter.67.cloned.1.call-update) | async-done | bytes 16400 | tf_op jit(solution)/shard_map/reduce_scatter | solution.py:525
  2239.3 154.5 %reduce-scatter.57.cloned.1.call-done = bf16[32,256]{1,0:T(8,128)(2,1)} async-done(((bf16[1024,256]{1,0:T(8,128)(2,1)}), bf16[32,256]{1,0:T(8,128)(2,1)}) %reduce-scatter.57.cloned.1.call-update) | async-done | bytes 16400 | tf_op jit(solution)/shard_map/reduce_scatter | solution.py:566
  2395.1 157.0 %reduce-scatter.55.cloned.1.call-done = bf16[32,256]{1,0:T(8,128)(2,1)} async-done(((bf16[1024,256]{1,0:T(8,128)(2,1)}), bf16[32,256]{1,0:T(8,128)(2,1)}) %reduce-scatter.55.cloned.1.call-update) | async-done | bytes 16400 | tf_op jit(solution)/shard_map/reduce_scatter | solution.py:563
  2553.4 157.0 %reduce-scatter.59.cloned.1.call-done = bf16[24,192]{1,0:T(8,128)(2,1)} async-done(((bf16[768,192]{1,0:T(8,128)(2,1)}), bf16[24,192]{1,0:T(8,128)(2,1)}) %reduce-scatter.59.cloned.1.call-update) | async-done | bytes 9232 | tf_op jit(solution)/shard_map/reduce_scatter | solution.py:513
  2711.8 159.5 %reduce-scatter.63.cloned.1.call-done = bf16[24,768]{1,0:T(8,128)(2,1)} async-done(((bf16[768,768]{1,0:T(8,128)(2,1)}), bf16[24,768]{1,0:T(8,128)(2,1)}) %reduce-scatter.63.cloned.1.call-update) | async-done | bytes 36880 | tf_op jit(solution)/shard_map/reduce_scatter | solution.py:519
  2872.7 159.1 %reduce-scatter.61.cloned.1.call-done = bf16[24,768]{1,0:T(8,128)(2,1)} async-done(((bf16[768,768]{1,0:T(8,128)(2,1)}), bf16[24,768]{1,0:T(8,128)(2,1)}) %reduce-scatter.61.cloned.1.call-update) | async-done | bytes 36880 | tf_op jit(solution)/shard_map/reduce_scatter | solution.py:516
  3033.2 155.5 %reduce-scatter.53.cloned.1.call-done = bf16[32,256]{1,0:T(8,128)(2,1)} async-done(((bf16[1024,256]{1,0:T(8,128)(2,1)}), bf16[32,256]{1,0:T(8,128)(2,1)}) %reduce-scatter.53.cloned.1.call-update) | async-done | bytes 16400 | tf_op jit(solution)/shard_map/reduce_scatter | solution.py:560
  3190.0 160.6 %reduce-scatter.65.cloned.1.call-done = bf16[32,3,256]{2,0,1:T(8,128)(2,1)} async-done(((bf16[1024,3,256]{2,0,1:T(8,128)(2,1)}), bf16[32,3,256]{2,0,1:T(8,128)(2,1)}) %reduce-scatter.65.cloned.1.call-update) | async-done | bytes 49168 | tf_op jit(solution)/shard_map/reduce_scatter | solution.py:522
  3352.2 128.6 %all-reduce.12 = (f32[2,256]{1,0:T(2,128)}, f32[1,768]{1,0:T(1,128)}, f32[2,256]{1,0:T(2,128)}, f32[1,256]{1,0:T(1,128)}, f32[2,192]{1,0:T(2,128)}, /*index=5*/f...) all-reduce(f32[2,256]{1,0:T(2,128)S(1)} %pad_maximum_fusion.24, ...), channel_id=1, replica_groups=mesh['rows'=32,'seq'=4] {'rows'}, use_global_device_ids=true, to_apply=%region_78.79 | all-reduce | flops 3968 | bytes 31744 | tf_op jit(solution)/shard_map/psum | solution.py:572
  3510.0 67.0 %all-reduce.39.cloned.1.call-done = bf16[3,144,1024]{2,1,0:T(8,128)(2,1)} async-done(((bf16[3,144,1024]{2,1,0:T(8,128)(2,1)}), bf16[3,144,1024]{2,1,0:T(8,128)(2,1)}) %all-reduce.39.cloned.1.call-update) | async-done | bytes 884752
  3609.7 136.7 %reduce-scatter.51.cloned.1.call-done = bf16[24,768]{1,0:T(8,128)(2,1)} async-done(((bf16[768,768]{1,0:T(8,128)(2,1)}), bf16[24,768]{1,0:T(8,128)(2,1)}) %reduce-scatter.51.cloned.1.call-update) | async-done | bytes 36880 | tf_op jit(solution)/shard_map/reduce_scatter | solution.py:554
  3747.9 158.5 %reduce-scatter.49.cloned.1.call-done = bf16[24,768]{1,0:T(8,128)(2,1)} async-done(((bf16[768,768]{1,0:T(8,128)(2,1)}), bf16[24,768]{1,0:T(8,128)(2,1)}) %reduce-scatter.49.cloned.1.call-update) | async-done | bytes 36880 | tf_op jit(solution)/shard_map/reduce_scatter | solution.py:551
  3907.8 329.8 %all-reduce.43.cloned.1.call-done = (bf16[768,3,256]{2,1,0:T(4,128)(2,1)}, bf16[1024,3,256]{2,1,0:T(4,128)(2,1)}, bf16[768,3,192]{2,0,1:T(8,128)(2,1)}) async-done(((bf16[768,3,256]{2,1,0:T(4,128)(2,1)}, bf16[1024,3,256]{2,1,0:T(4,128)(2,1)}, bf16[768,3,192]{2,0,1:T(8,128)(2,1)}), (bf16[768,3,256]{2,1,0:T(4,128)(2,1)}, bf16[1024,3,256]{2,1,0:T(4,128)(2,1)}, ...) | async-done | bytes 3637264
  4242.0 164.5 %all-reduce.41.cloned.1.call-done = (f32[4,768]{1,0:T(4,128)}, f32[2,768]{1,0:T(2,128)}, f32[4,1024]{1,0:T(4,128)}, f32[2,1024]{1,0:T(2,128)}, f32[4,768]{1,0:T(...) async-done(((f32[4,768]{1,0:T(4,128)}, f32[2,768]{1,0:T(2,128)}, f32[4,1024]{1,0:T(4,128)}, f32[2,1024]{1,0:T(2,128)}, f32[4,768]{1,0:T(4,128)}, ...) | async-done | bytes 86032 | tf_op jit(solution)/shard_map/psum | solution.py:587
  (896 shorter events, 653.3 us)
Async XLA Ops:
  7.3 136.8 %all-gather.10.cloned.1.call-start = ((), (), s32[]{:S(2)}) async-start(), calls=%async_computation.22 | async-start | bytes 1216512 | tf_op jit(solution)/shard_map/all_gather | solution.py:427
  8.0 290.3 %all-gather.8.cloned.1.call-start = ((), (), s32[]{:S(2)}) async-start(), calls=%async_computation.21 | async-start | bytes 1622016 | tf_op jit(solution)/shard_map/all_gather | solution.py:431
  8.7 502.8 %all-reduce.25.cloned.1.call-start = ((), (), s32[]{:S(2)}) async-start(), calls=%async_computation.49 | async-start | bytes 1769472
  304.2 645.0 %reduce-scatter.31.cloned.1.call-start = ((), (), s32[]{:S(2)}) async-start(), calls=%async_computation.23 | async-start | bytes 737280 | tf_op jit(solution)/shard_map/reduce_scatter | solution.py:39
  376.7 644.3 %all-gather.12.cloned.1.call-start = ((), (), s32[]{:S(2)}) async-start(), calls=%async_computation.24 | async-start | bytes 1216512 | tf_op jit(solution)/shard_map/all_gather | solution.py:429
  377.3 646.9 %all-gather.14.cloned.1.call-start = ((), (), s32[]{:S(2)}) async-start(), calls=%async_computation.25 | async-start | bytes 1216512 | tf_op jit(solution)/shard_map/all_gather | solution.py:430
  377.9 649.7 %all-reduce.27.cloned.1.call-start = ((), (), s32[]{:S(2)}) async-start(), calls=%async_computation.50 | async-start | bytes 1769472
  592.4 450.0 %all-gather.20.cloned.1.call-start = ((), (), s32[]{:S(2)}) async-start(), calls=%async_computation.31 | async-start | bytes 1622016 | tf_op jit(solution)/shard_map/all_gather | solution.py:470
  593.2 459.1 %reduce-scatter.33.cloned.1.call-start = ((), (), s32[]{:S(2)}) async-start(), calls=%async_computation.26 | async-start | bytes 737280 | tf_op jit(solution)/shard_map/reduce_scatter | solution.py:39
  1120.2 202.5 %all-gather.16.cloned.1.call-start = ((), (), s32[]{:S(2)}) async-start(), calls=%async_computation.28 | async-start | bytes 1216512 | tf_op jit(solution)/shard_map/all_gather | solution.py:468
  1120.9 354.4 %all-gather.18.cloned.1.call-start = ((), (), s32[]{:S(2)}) async-start(), calls=%async_computation.29 | async-start | bytes 1216512 | tf_op jit(solution)/shard_map/all_gather | solution.py:469
  1121.5 422.7 %all-reduce.33.cloned.1.call-start = ((), (), s32[]{:S(2)}) async-start(), calls=%async_computation.53 | async-start | bytes 1769472
  1209.1 369.3 %reduce-scatter.37.cloned.1.call-start = ((), (), s32[]{:S(2)}) async-start(), calls=%async_computation.30 | async-start | bytes 737280 | tf_op jit(solution)/shard_map/reduce_scatter | solution.py:39
  1478.7 143.7 %all-reduce.35.cloned.1.call-start = ((), (), s32[]{:S(2)}) async-start(), calls=%async_computation.54 | async-start | bytes 1769472
  1594.8 110.3 %reduce-scatter.41.cloned.1.call-start = ((), (), s32[]{:S(2)}) async-start(), calls=%async_computation.33 | async-start | bytes 737280 | tf_op jit(solution)/shard_map/reduce_scatter | solution.py:57
  1720.5 198.1 %reduce-scatter.71.cloned.1.call-start = ((), (), s32[]{:S(2)}) async-start(), calls=%async_computation.48 | async-start | bytes 540672 | tf_op jit(solution)/shard_map/reduce_scatter | solution.py:531
  1723.7 353.3 %reduce-scatter.69.cloned.1.call-start = ((), (), s32[]{:S(2)}) async-start(), calls=%async_computation.47 | async-start | bytes 540672 | tf_op jit(solution)/shard_map/reduce_scatter | solution.py:528
  1726.2 509.0 %reduce-scatter.67.cloned.1.call-start = ((), (), s32[]{:S(2)}) async-start(), calls=%async_computation.46 | async-start | bytes 540672 | tf_op jit(solution)/shard_map/reduce_scatter | solution.py:525
  1729.2 664.6 %reduce-scatter.57.cloned.1.call-start = ((), (), s32[]{:S(2)}) async-start(), calls=%async_computation.41 | async-start | bytes 540672 | tf_op jit(solution)/shard_map/reduce_scatter | solution.py:566
  1732.0 820.1 %reduce-scatter.55.cloned.1.call-start = ((), (), s32[]{:S(2)}) async-start(), calls=%async_computation.40 | async-start | bytes 540672 | tf_op jit(solution)/shard_map/reduce_scatter | solution.py:563
  1734.9 975.6 %reduce-scatter.59.cloned.1.call-start = ((), (), s32[]{:S(2)}) async-start(), calls=%async_computation.42 | async-start | bytes 405504 | tf_op jit(solution)/shard_map/reduce_scatter | solution.py:513
  1736.4 1135.0 %reduce-scatter.63.cloned.1.call-start = ((), (), s32[]{:S(2)}) async-start(), calls=%async_computation.44 | async-start | bytes 1216512 | tf_op jit(solution)/shard_map/reduce_scatter | solution.py:519
  1739.7 1292.1 %reduce-scatter.61.cloned.1.call-start = ((), (), s32[]{:S(2)}) async-start(), calls=%async_computation.43 | async-start | bytes 1216512 | tf_op jit(solution)/shard_map/reduce_scatter | solution.py:516
  1742.8 1445.9 %reduce-scatter.53.cloned.1.call-start = ((), (), s32[]{:S(2)}) async-start(), calls=%async_computation.39 | async-start | bytes 540672 | tf_op jit(solution)/shard_map/reduce_scatter | solution.py:560
  1770.2 1580.5 %reduce-scatter.65.cloned.1.call-start = ((), (), s32[]{:S(2)}) async-start(), calls=%async_computation.45 | async-start | bytes 1622016 | tf_op jit(solution)/shard_map/reduce_scatter | solution.py:522
  1773.9 1734.8 %reduce-scatter.47.cloned.1.call-start = ((), (), s32[]{:S(2)}) async-start(), calls=%async_computation.36 | async-start | bytes 405504 | tf_op jit(solution)/shard_map/reduce_scatter | solution.py:548
  1798.0 1779.1 %all-reduce.39.cloned.1.call-start = ((), (), s32[]{:S(2)}) async-start(), calls=%async_computation.56 | async-start | bytes 1769472
  1806.6 1801.4 %reduce-scatter.45.cloned.1.call-start = ((), (), s32[]{:S(2)}) async-start(), calls=%async_computation.35 | async-start | bytes 737280 | tf_op jit(solution)/shard_map/reduce_scatter | solution.py:57
  1820.1 1926.3 %reduce-scatter.51.cloned.1.call-start = ((), (), s32[]{:S(2)}) async-start(), calls=%async_computation.38 | async-start | bytes 1216512 | tf_op jit(solution)/shard_map/reduce_scatter | solution.py:554
  1823.4 2082.9 %reduce-scatter.49.cloned.1.call-start = ((), (), s32[]{:S(2)}) async-start(), calls=%async_computation.37 | async-start | bytes 1216512 | tf_op jit(solution)/shard_map/reduce_scatter | solution.py:551
  1827.5 2410.1 %all-reduce.43.cloned.1.call-start = ((), (), s32[]{:S(2)}) async-start(), calls=%async_computation.58 | async-start | bytes 9699328
  1844.1 2562.3 %all-reduce.41.cloned.1.call-start = ((), (), s32[]{:S(2)}) async-start(), calls=%async_computation.57 | async-start | bytes 172032 | tf_op jit(solution)/shard_map/psum | solution.py:587
  (258 other events, 35597.6 us)
Sparse Core Ops, SparseCore 0:
  9.7 134.2 all-gather.9
  145.7 152.6 all-gather.7
  304.4 65.6 all-reduce.24
  376.8 60.1 reduce-scatter.30
  438.5 130.3 all-gather.11
  570.5 152.2 all-gather.13
  725.3 65.5 all-reduce.26
  792.5 130.9 all-gather.19
  1054.6 44.0 all-reduce.28
  1117.0 43.5 all-reduce.30
  1192.9 129.6 all-gather.15
  1324.1 151.1 all-gather.17
  1477.7 66.4 all-reduce.32
  1578.4 43.8 all-reduce.34
  1707.5 44.0 all-reduce.36
  1754.2 28.1 reduce-scatter.42
  1784.7 133.8 reduce-scatter.70
  1921.1 155.8 reduce-scatter.68
  2079.2 156.0 reduce-scatter.66
  2237.7 156.0 reduce-scatter.56
  2396.0 156.0 reduce-scatter.54
  2554.4 156.0 reduce-scatter.58
  2712.8 158.4 reduce-scatter.62
  2873.8 157.9 reduce-scatter.60
  3034.0 154.6 reduce-scatter.52
  3191.2 159.4 reduce-scatter.64
  3353.0 155.6 reduce-scatter.46
  3511.3 65.7 all-reduce.38
  3610.5 135.9 reduce-scatter.50
  3748.7 157.6 reduce-scatter.48
  3909.2 328.3 all-reduce.42
  4246.8 159.5 all-reduce.40
  (6 shorter events, 164.5 us)
where the time goes:
time: 4440 us; the launch traced here: 4420 us
  waiting for transfers between devices  3070 us (69%)
  blocking collectives  1070 us (24%)
  matrix products  140 us (3%)
  other arithmetic  76.5 us (2%)
  local copies, waits for them, and re-layouts  50.4 us (1%)
    unnamed x47, waiting for transfers between devices  573 us
    psum x1, waiting for transfers between devices, on_device(): lax.psum((cross_vecs[0][0], cross_vecs[0][1], cross_vecs[1][0], cross_vec...  164 us
    reduce_scatter x1, waiting for transfers between devices, on_device(): lax.psum_scatter(self_mats[1][0].astype(jnp.bfloat16), 'rows', scatter_di...  161 us
    reduce_scatter x1, waiting for transfers between devices, on_device(): lax.psum_scatter(self_mats[0][3].astype(jnp.bfloat16), 'rows', scatter_di...  160 us
    reduce_scatter x1, waiting for transfers between devices, on_device(): lax.psum_scatter(self_mats[0][2].astype(jnp.bfloat16), 'rows', scatter_di...  159 us
    reduce_scatter x1, waiting for transfers between devices, on_device(): lax.psum_scatter(cross_mats[0][2].astype(jnp.bfloat16), 'rows', scatter_d...  159 us
    reduce_scatter x1, waiting for transfers between devices, on_device(): lax.psum_scatter(self_mats[0][1].astype(jnp.bfloat16), 'rows', scatter_di...  157 us
    reduce_scatter x1, waiting for transfers between devices, on_device(): lax.psum_scatter(self_mats[1][2].astype(jnp.bfloat16), 'rows', scatter_di...  157 us
  transfers between devices with their start and end apart: 38, of which 30 were waited for; matrix products, arithmetic and copies ran while one was open for 5% of the time, Pallas kernels for 0%

commit v1 on v0

--- a/solution.py
+++ b/solution.py
@@ -1,6 +1,8 @@
 import jax
 import jax.numpy as jnp
 from jax import lax
+from jax.experimental import pallas as pl
+from jax.experimental.pallas import tpu as pltpu
 from jax.sharding import PartitionSpec as P
 
 DT = 768
@@ -13,6 +15,231 @@
 
 epsilon = 1e-05
 masked_value = -1000000000.0
+
+
+MESH = pl.DeviceIdType.MESH
+VMEM = pltpu.VMEM
+DMA = pltpu.SemaphoreType.DMA
+
+
+class Place:
+    def __init__(self):
+        r = lax.axis_index("rows")
+        s = lax.axis_index("seq")
+        self.r, self.s = r, s
+        self.x, self.z, self.y = r // 8, (r // 4) % 2, r % 4
+        self.zh, self.c = s // 2, s % 2
+
+    def dev(self, x, z, y):
+        return ((x * 2 + z) * 4 + y, self.s)
+
+    def along(self, axis, step):
+        x, z, y = self.x, self.z, self.y
+        if axis == "x":
+            return self.dev((x + step) % 4, z, y)
+        if axis == "y":
+            return self.dev(x, z, (y + step) % 4)
+        return self.dev(x, 1 - z, y)
+
+
+def greet(devices):
+    barrier = pltpu.get_barrier_semaphore()
+    for device in devices:
+        pl.semaphore_signal(barrier, inc=1, device_id=device, device_id_type=MESH)
+    pl.semaphore_wait(barrier, len(devices))
+
+
+def push(src, dst, sems, k, device):
+    copy = pltpu.make_async_remote_copy(
+        src_ref=src, dst_ref=dst, send_sem=sems.at[0, k], recv_sem=sems.at[1, k],
+        device_id=device, device_id_type=MESH)
+    copy.start()
+    return copy
+
+
+def gather_steps(me, own, buf, sems, order):
+    x, z, y = me.x, me.z, me.y
+    sent = []
+    first = push(own, buf.at[x, z, y], sems, 0, me.along("z", 1))
+    local = pltpu.make_async_copy(own, buf.at[x, z, y], sems.at[0, 9])
+    local.start()
+    yield
+    local.wait()
+    first.wait()
+    k = 1
+    for stage, axis in enumerate(order):
+        if axis == "x":
+            def view(step, half):
+                at = (x + step) % 4
+                if stage == 0:
+                    return buf.at[at, :, y] if half is None else buf.at[at, half, y]
+                return buf.at[at] if half is None else buf.at[at, :, pl.ds(2 * half, 2)]
+        else:
+            def view(step, half):
+                at = (y + step) % 4
+                if stage == 0:
+                    return buf.at[x, :, at] if half is None else buf.at[x, half, at]
+                return buf.at[:, :, at] if half is None else buf.at[pl.ds(2 * half, 2), :, at]
+        right, left = me.along(axis, 1), me.along(axis, 3)
+        to_right = push(view(0, None), view(0, None), sems, k, right)
+        to_left = push(view(0, None), view(0, None), sems, k + 1, left)
+        yield
+        to_right.wait_recv()
+        on_right = push(view(3, 0), view(3, 0), sems, k + 2, right)
+        to_left.wait_recv()
+        on_left = push(view(1, 1), view(1, 1), sems, k + 3, left)
+        yield
+        on_right.wait_recv()
+        on_left.wait_recv()
+        sent += [to_right, to_left, on_right, on_left]
+        k += 4
+    for copy in sent:
+        copy.wait_send()
+
+
+def run_together(steps):
+    steps = list(steps)
+    while steps:
+        alive = []
+        for step in steps:
+            try:
+                next(step)
+                alive.append(step)
+            except StopIteration:
+                pass
+        steps = alive
+
+
+def gather_kernel(orders, *refs):
+    n = len(orders)
+    owns, bufs, sems = refs[:n], refs[n:2 * n], refs[2 * n:]
+    me = Place()
+    greet([me.along("z", 1), me.along("x", 1), me.along("x", 3), me.along("y", 1), me.along("y", 3)])
+    run_together(gather_steps(me, owns[i], bufs[i], sems[i], orders[i]) for i in range(n))
+
+
+def gather_all(packs, orders, collective_id=0):
+    return pl.pallas_call(
+        lambda *refs: gather_kernel(orders, *refs),
+        out_shape=[jax.ShapeDtypeStruct((4, 2, 4) + p.shape, p.dtype) for p in packs],
+        in_specs=[pl.BlockSpec(memory_space=pl.ANY)] * len(packs),
+        out_specs=[pl.BlockSpec(memory_space=pl.ANY)] * len(packs),
+        scratch_shapes=[DMA((2, 10))] * len(packs),
+        compiler_params=pltpu.CompilerParams(collective_id=collective_id, has_side_effects=True),
+    )(*packs)
+
+
+def add_slabs(me, dst, src, count):
+    def one(i, carry):
+        at = dst(i)
+        at[...] = (at[...].astype(jnp.float32) + src(i)[...].astype(jnp.float32)).astype(at.dtype)
+        return carry
+    lax.fori_loop(0, count, one, 0)
+
+
+def reduce_steps(me, buf, out, halves, chunks, small_halves, small_chunks, last, sems, order):
+    x, z, y = me.x, me.z, me.y
+    sent = []
+    k = 0
+    for stage, axis in enumerate(order):
+        half_in, chunk_in = (halves, chunks) if stage == 0 else (small_halves, small_chunks)
+        place = x if axis == "x" else y
+        if axis == "x":
+            def view(step, half=None):
+                at = (x + step) % 4
+                if stage == 0:
+                    return buf.at[at] if half is None else buf.at[at, :, pl.ds(2 * half, 2)]
+                return buf.at[at, :, y] if half is None else buf.at[at, half, y]
+        else:
+            def view(step, half=None):
+                at = (y + step) % 4
+                if stage == 0:
+                    return buf.at[:, :, at] if half is None else buf.at[pl.ds(2 * half, 2), :, at]
+                return buf.at[x, :, at] if half is None else buf.at[x, half, at]
+        right, left = me.along(axis, 1), me.along(axis, 3)
+        a = push(view(2, 0), half_in.at[0], sems, k, right)
+        b = push(view(2, 1), half_in.at[1], sems, k + 1, left)
+        yield
+        if stage == 0:
+            def half_slab(step, half):
+                at = (place + step) % 4
+                if axis == "x":
+                    return lambda i: buf.at[at, i // 2, 2 * half + i % 2]
+                return lambda i: buf.at[2 * half + i // 2, i % 2, at]
+
+            def full_slab(i):
+                return buf.at[x, i // 4, i % 4] if axis == "x" else buf.at[i // 2, i % 2, y]
+            n_half, n_full = 4, 8
+        else:
+            def half_slab(step, half):
+                at = (place + step) % 4
+                return lambda i: buf.at[at, half, y] if axis == "x" else buf.at[x, half, at]
+
+            def full_slab(i):
+                return buf.at[x, i, y]
+            n_half, n_full = 1, 2
+
+        def in_slab(ref, d):
+            if stage == 1:
+                return (lambda i: ref.at[d]) if ref is half_in else (lambda i: ref.at[d, i])
+            wide = ref.shape[2]
+            return lambda i: ref.at[d, i // wide, i % wide]
+        a.wait_recv()
+        add_slabs(me, half_slab(1, 0), in_slab(half_in, 0), n_half)
+        c = push(view(1), chunk_in.at[0], sems, k + 2, right)
+        b.wait_recv()
+        add_slabs(me, half_slab(3, 1), in_slab(half_in, 1), n_half)
+        d = push(view(3), chunk_in.at[1], sems, k + 3, left)
+        yield
+        c.wait_recv()
+        add_slabs(me, full_slab, in_slab(chunk_in, 0), n_full)
+        d.wait_recv()
+        add_slabs(me, full_slab, in_slab(chunk_in, 1), n_full)
+        sent += [a, b, c, d]
+        k += 4
+    e = push(buf.at[x, 1 - z, y], last, sems, k, me.along("z", 1))
+    yield
+    e.wait_recv()
+    out[...] = buf[x, z, y].astype(jnp.float32) + last[...].astype(jnp.float32)
+    sent.append(e)
+    for copy in sent:
+        copy.wait_send()
+
+
+def reduce_scratch(order, rows, cols):
+    lead = (2, 4) if order[0] == "x" else (4, 2)
+    bf = jnp.bfloat16
+    return [VMEM((2, 2, 2, rows, cols), bf), VMEM((2,) + lead + (rows, cols), bf),
+            VMEM((2, rows, cols), bf), VMEM((2, 2, rows, cols), bf), VMEM((rows, cols), bf), DMA((2, 9))]
+
+
+def reduce_kernel(orders, *refs):
+    n = len(orders)
+    ins, outs, scratch = refs[:n], refs[n:2 * n], refs[2 * n:]
+    me = Place()
+    copies = []
+    for i in range(n):
+        copies.append(pltpu.make_async_copy(ins[i], scratch[7 * i], scratch[7 * i + 6].at[0, 0]))
+        copies[-1].start()
+    greet([me.along("z", 1), me.along("x", 1), me.along("x", 3), me.along("y", 1), me.along("y", 3)])
+    for copy in copies:
+        copy.wait()
+    run_together(reduce_steps(me, scratch[7 * i], outs[i], *scratch[7 * i + 1:7 * i + 7], orders[i]) for i in range(n))
+
+
+def reduce_all(packs, orders, collective_id=1):
+    scratch = []
+    for p, order in zip(packs, orders):
+        scratch += [VMEM(p.shape, p.dtype)] + reduce_scratch(order, p.shape[3], p.shape[4])
+    return pl.pallas_call(
+        lambda *refs: reduce_kernel(orders, *refs),
+        out_shape=[jax.ShapeDtypeStruct(p.shape[3:], jnp.float32) for p in packs],
+        in_specs=[pl.BlockSpec(memory_space=pl.ANY)] * len(packs),
+        out_specs=[pl.BlockSpec(memory_space=pltpu.VMEM)] * len(packs),
+        scratch_shapes=scratch,
+        compiler_params=pltpu.CompilerParams(collective_id=collective_id, has_side_effects=True,
+                                             vmem_limit_bytes=60 * 1024 * 1024),
+    )(*packs)
 
 
 def segments(lengths, positions_total):
@@ -368,6 +595,33 @@
             )
         )
     return (next_grads, matrices, columns, vectors)
+
+
+def pack_shard(proj, out, up, down):
+    return jnp.concatenate([proj.reshape(proj.shape[0], -1), out, up, down], axis=1)
+
+
+def cuts_of(proj, out, up):
+    a = proj.shape[2]
+    return (3 * a, 4 * a, 4 * a + up.shape[1])
+
+
+def unpack_whole(gathered, proj, out, up, down):
+    whole = gathered.reshape(-1, gathered.shape[-1])
+    a, b, c = cuts_of(proj, out, up)
+    return (whole[:, :a].reshape(-1, 3, proj.shape[2]), whole[:, a:b], whole[:, b:c], whole[:, c:])
+
+
+def pack_whole(mats):
+    whole = jnp.concatenate(
+        [mats[0].reshape(mats[0].shape[0], -1), mats[1], mats[2], mats[3]], axis=1
+    ).astype(jnp.bfloat16)
+    return whole.reshape(4, 2, 4, whole.shape[0] // 32, whole.shape[1])
+
+
+def unpack_shard(total, proj, out, up):
+    a, b, c = cuts_of(proj, out, up)
+    return (total[:, :a].reshape(proj.shape), total[:, a:b], total[:, b:c], total[:, c:])
 
 
 def on_device(
@@ -423,15 +677,16 @@
     )
     cross_heads = (DC // HEADS_CROSS, DC // HEADS_CROSS)
     self_heads = (DT // HEADS_TEXT, DI // HEADS_IMAGE)
+    packs = [
+        pack_shard(cross_text_proj, cross_text_out, cross_text_up, cross_text_down),
+        pack_shard(cross_image_proj, cross_image_out, cross_image_up, cross_image_down),
+        pack_shard(self_text_proj, self_text_out, self_text_up, self_text_down),
+        pack_shard(self_image_proj, self_image_out, self_image_up, self_image_down),
+    ]
+    gathered = gather_all(packs, ["xy", "yx", "xy", "yx"])
     cross_fetched = (
-        lax.all_gather(cross_text_proj, "rows", axis=0, tiled=True),
-        lax.all_gather(cross_text_out, "rows", axis=0, tiled=True),
-        lax.all_gather(cross_text_up, "rows", axis=0, tiled=True),
-        lax.all_gather(cross_text_down, "rows", axis=0, tiled=True),
-        lax.all_gather(cross_image_proj, "rows", axis=0, tiled=True),
-        lax.all_gather(cross_image_out, "rows", axis=0, tiled=True),
-        lax.all_gather(cross_image_up, "rows", axis=0, tiled=True),
-        lax.all_gather(cross_image_down, "rows", axis=0, tiled=True),
+        unpack_whole(gathered[0], cross_text_proj, cross_text_out, cross_text_up, cross_text_down)
+        + unpack_whole(gathered[1], cross_image_proj, cross_image_out, cross_image_up, cross_image_down)
     )
     cross_blocks = [
         (
@@ -463,14 +718,8 @@
         True,
     )
     self_fetched = (
-        lax.all_gather(self_text_proj, "rows", axis=0, tiled=True),
-        lax.all_gather(self_text_out, "rows", axis=0, tiled=True),
-        lax.all_gather(self_text_up, "rows", axis=0, tiled=True),
-        lax.all_gather(self_text_down, "rows", axis=0, tiled=True),
-        lax.all_gather(self_image_proj, "rows", axis=0, tiled=True),
-        lax.all_gather(self_image_out, "rows", axis=0, tiled=True),
-        lax.all_gather(self_image_up, "rows", axis=0, tiled=True),
-        lax.all_gather(self_image_down, "rows", axis=0, tiled=True),
+        unpack_whole(gathered[2], self_text_proj, self_text_out, self_text_up, self_text_down)
+        + unpack_whole(gathered[3], self_image_proj, self_image_out, self_image_up, self_image_down)
     )
     self_blocks = [
         (
@@ -506,32 +755,6 @@
         False,
     )
     self_mats = self_back[1]
-    self_sums = (
-        lax.psum_scatter(
-            self_mats[0][0].astype(jnp.bfloat16), "rows", scatter_dimension=0, tiled=True
-        ).astype(jnp.float32),
-        lax.psum_scatter(
-            self_mats[0][1].astype(jnp.bfloat16), "rows", scatter_dimension=0, tiled=True
-        ).astype(jnp.float32),
-        lax.psum_scatter(
-            self_mats[0][2].astype(jnp.bfloat16), "rows", scatter_dimension=0, tiled=True
-        ).astype(jnp.float32),
-        lax.psum_scatter(
-            self_mats[0][3].astype(jnp.bfloat16), "rows", scatter_dimension=0, tiled=True
-        ).astype(jnp.float32),
-        lax.psum_scatter(
-            self_mats[1][0].astype(jnp.bfloat16), "rows", scatter_dimension=0, tiled=True
-        ).astype(jnp.float32),
-        lax.psum_scatter(
-            self_mats[1][1].astype(jnp.bfloat16), "rows", scatter_dimension=0, tiled=True
-        ).astype(jnp.float32),
-        lax.psum_scatter(
-            self_mats[1][2].astype(jnp.bfloat16), "rows", scatter_dimension=0, tiled=True
-        ).astype(jnp.float32),
-        lax.psum_scatter(
-            self_mats[1][3].astype(jnp.bfloat16), "rows", scatter_dimension=0, tiled=True
-        ).astype(jnp.float32),
-    )
     cross_back = backward_block(
         (self_back[0][0], self_back[0][1]),
         cross_stored,
@@ -541,31 +764,17 @@
         True,
     )
     cross_mats = cross_back[1]
+    totals = reduce_all(
+        [pack_whole(cross_mats[0]), pack_whole(cross_mats[1]), pack_whole(self_mats[0]), pack_whole(self_mats[1])],
+        ["yx", "xy", "yx", "xy"],
+    )
     cross_sums = (
-        lax.psum_scatter(
-            cross_mats[0][0].astype(jnp.bfloat16), "rows", scatter_dimension=0, tiled=True
-        ).astype(jnp.float32),
-        lax.psum_scatter(
-            cross_mats[0][1].astype(jnp.bfloat16), "rows", scatter_dimension=0, tiled=True
-        ).astype(jnp.float32),
-        lax.psum_scatter(
-            cross_mats[0][2].astype(jnp.bfloat16), "rows", scatter_dimension=0, tiled=True
-        ).astype(jnp.float32),
-        lax.psum_scatter(
-            cross_mats[0][3].astype(jnp.bfloat16), "rows", scatter_dimension=0, tiled=True
-        ).astype(jnp.float32),
-        lax.psum_scatter(
-            cross_mats[1][0].astype(jnp.bfloat16), "rows", scatter_dimension=0, tiled=True
-        ).astype(jnp.float32),
-        lax.psum_scatter(
-            cross_mats[1][1].astype(jnp.bfloat16), "rows", scatter_dimension=0, tiled=True
-        ).astype(jnp.float32),
-        lax.psum_scatter(
-            cross_mats[1][2].astype(jnp.bfloat16), "rows", scatter_dimension=0, tiled=True
-        ).astype(jnp.float32),
-        lax.psum_scatter(
-            cross_mats[1][3].astype(jnp.bfloat16), "rows", scatter_dimension=0, tiled=True
-        ).astype(jnp.float32),
+        unpack_shard(totals[0], cross_text_proj, cross_text_out, cross_text_up)
+        + unpack_shard(totals[1], cross_image_proj, cross_image_out, cross_image_up)
+    )
+    self_sums = (
+        unpack_shard(totals[2], self_text_proj, self_text_out, self_text_up)
+        + unpack_shard(totals[3], self_image_proj, self_image_out, self_image_up)
     )
     cross_cols = cross_back[2]
     self_cols = self_back[2]

time: 4440 us -> 1200 us (0.27)
  waiting for transfers between devices: 3070 us -> 382 us
  blocking collectives: 1070 us -> 307 us
  Pallas kernels: 0 us -> 180 us
  local copies, waits for them, and re-layouts: 50.4 us -> 103 us
    reduce_scatter x13 -> x0, waiting for transfers between devices: 1810 us -> none  [the longest x1 161 us: on_device(): lax.psum_scatter(self_mats[1][0].astype(jnp.bfloat16), 'rows', scatter_di...]
    all_gather x9 -> x0, blocking collectives: 626 us -> none  [the longest x1 78.4 us: on_device(): lax.all_gather(self_text_proj, 'rows', axis=0, tiled=True)]
    all_gather x7 -> x0, waiting for transfers between devices: 427 us -> none  [the longest x1 152 us: on_device(): lax.all_gather(cross_image_proj, 'rows', axis=0, tiled=True)]
    unnamed x47 -> x25, waiting for transfers between devices: 573 us -> 177 us
    pallas_call x0 -> x2, Pallas kernels: none -> 180 us  [the longest x1 91.2 us: reduce_all(): pl.pallas_call(lambda *refs: reduce_kernel(orders, *refs), out_shape=[jax...]
    all_gather x4, blocking collectives: 126 us -> 50.5 us  [spread_tokens(): lax.all_gather(image_part, 'seq', axis=1, tiled=True)]
    all_gather x4, blocking collectives: 99.1 us -> 39.2 us  [spread_tokens(): lax.all_gather(text_part, 'seq', axis=1, tiled=True)]
    reduce_scatter x4, waiting for transfers between devices: 67.2 us -> 17 us  [gradients_from_partials(): lax.psum_scatter(text_part.astype(jnp.bfloat16), 'seq', scatter_dimension...]
  transfers between devices with their start and end apart: 38 -> 17, of which waited for: 30 -> 14; matrix products, arithmetic and copies ran while one was open for 5% -> 20% of each run, Pallas kernels for 0% -> 8%
where the time goes in v1:
time: 1200 us; the launch traced here: 1190 us
  waiting for transfers between devices  382 us (32%)
  blocking collectives  307 us (26%)
  Pallas kernels  180 us (15%)
  matrix products  137 us (11%)
  local copies, waits for them, and re-layouts  103 us (9%)
  other arithmetic  63.1 us (5%)
  between operations  17.9 us (1%)
    unnamed x25, waiting for transfers between devices  177 us
    psum x1, waiting for transfers between devices, on_device(): lax.psum((cross_vecs[0][0], cross_vecs[0][1], cross_vecs[1][0], cross_vec...  160 us
    psum x1, blocking collectives, on_device(): lax.psum((cross_cols[0][0], cross_cols[0][1], cross_cols[1][0], cross_col...  126 us
    pallas_call x1, Pallas kernels, reduce_all(): pl.pallas_call(lambda *refs: reduce_kernel(orders, *refs), out_shape=[jax...  91.2 us
    pallas_call x1, Pallas kernels, gather_all(): pl.pallas_call(lambda *refs: gather_kernel(orders, *refs), out_shape=[jax...  89 us
    all_gather x4, blocking collectives, spread_tokens(): lax.all_gather(image_part, 'seq', axis=1, tiled=True)  50.5 us
    all_gather x4, blocking collectives, spread_gradients(): lax.all_gather(image_part, 'seq', axis=1, tiled=True)  50.1 us
    all_gather x4, blocking collectives, spread_gradients(): lax.all_gather(text_part, 'seq', axis=1, tiled=True)  40.9 us
  transfers between devices with their start and end apart: 17, of which 14 were waited for; matrix products, arithmetic and copies ran while one was open for 20% of the time, Pallas kernels for 8%

profile of v1, /device:TPU:1, one launch (start us, length us, event | category | flops | bytes accessed | tf_op | source)
XLA Modules:
  0.0 1191.5 jit_solution(18102397959204036008)
XLA Ops:
  14.5 11.6 all_gather.49
  26.1 12.8 %all_gather.48 = bf16[3,144,1024]{2,0,1:T(4,128)(2,1)} all-gather(bf16[3,36,1024]{2,0,1:T(4,128)(2,1)S(1)} %copy.338), channel_id=1, replica_groups=mesh['rows'=32,'seq'=4] {'seq'}, dimensions={1}, use_global_device_ids=true | all-gather | bytes 1105920 | tf_op jit(solution)/shard_map/all_gather | solution.py:260
  41.0 89.0 %shard_map.637 = (bf16[4,2,4,24,2560]{4,3,2,1,0:T(8,128)(2,1)}, bf16[4,2,4,32,1536]{4,3,2,1,0:T(8,128)(2,1)}, bf16[4,2,4,24,2304]{4,3,2,1,0:T(8,128)(2,1)}, bf16[4,2,4,32,1536]{4,3,2,1,0:T(8,128)(2,1)}) custom-call(bf16[24,2560]{1,0:T(8,128)(2,1)} %pad_maximum_fusion.15.refs_0_, bf16[32,1536]{1,0:T(8,128)(2,1)} %get-tuple-element.370.refs_1_, ...), custom_call_target="tpu_custom_call" | custom-call | tf_op jit(solution)/shard_map/pallas_call | solution.py:122
  161.4 26.6 %all-reduce.20.cloned.1.call-done = bf16[3,144,1024]{2,1,0:T(8,128)(2,1)} async-done(((bf16[3,144,1024]{2,1,0:T(8,128)(2,1)}), bf16[3,144,1024]{2,1,0:T(8,128)(2,1)}) %all-reduce.20.cloned.1.call-update) | async-done | bytes 884752
  191.0 12.8 %all_gather.53 = bf16[3,144,1024]{2,0,1:T(4,128)(2,1)S(1)} all-gather(bf16[3,36,1024]{2,0,1:T(4,128)(2,1)S(1)} %copy.353), channel_id=1, replica_groups=mesh['rows'=32,'seq'=4] {'seq'}, dimensions={1}, use_global_device_ids=true | all-gather | bytes 1105920 | tf_op jit(solution)/shard_map/all_gather | solution.py:260
  209.2 9.6 reduce-scatter.17.cloned.1.call-done
  222.0 9.2 all_gather.50
  237.3 28.1 %all-reduce.22.cloned.1.call-done = bf16[3,144,1024]{2,1,0:T(8,128)(2,1)} async-done(((bf16[3,144,1024]{2,1,0:T(8,128)(2,1)}), bf16[3,144,1024]{2,1,0:T(8,128)(2,1)}) %all-reduce.22.cloned.1.call-update) | async-done | bytes 884752
  267.4 12.5 %all_gather.54 = bf16[3,144,1024]{2,0,1:T(4,128)(2,1)S(1)} all-gather(bf16[3,36,1024]{2,0,1:T(4,128)(2,1)S(1)} %copy.355), channel_id=1, replica_groups=mesh['rows'=32,'seq'=4] {'seq'}, dimensions={1}, use_global_device_ids=true | all-gather | bytes 1105920 | tf_op jit(solution)/shard_map/all_gather | solution.py:260
  286.4 9.7 reduce-scatter.19.cloned.1.call-done
  297.6 9.2 all_gather.51
  307.6 34.9 %all-reduce.24.cloned.1.call-done = bf16[3,144,1024]{2,1,0:T(8,128)(2,1)} async-done(((bf16[3,144,1024]{2,1,0:T(8,128)(2,1)}), bf16[3,144,1024]{2,1,0:T(8,128)(2,1)}) %all-reduce.24.cloned.1.call-update) | async-done | bytes 884752
  344.4 12.4 %all_gather.55 = bf16[3,144,1024]{2,0,1:T(4,128)(2,1)S(1)} all-gather(bf16[3,36,1024]{2,0,1:T(4,128)(2,1)S(1)} %copy.364), channel_id=1, replica_groups=mesh['rows'=32,'seq'=4] {'seq'}, dimensions={1}, use_global_device_ids=true | all-gather | bytes 1105920 | tf_op jit(solution)/shard_map/all_gather | solution.py:260
  366.3 39.7 %all-reduce.26.cloned.1.call-done = bf16[3,144,1024]{2,1,0:T(8,128)(2,1)} async-done(((bf16[3,144,1024]{2,1,0:T(8,128)(2,1)}), bf16[3,144,1024]{2,1,0:T(8,128)(2,1)}) %all-reduce.26.cloned.1.call-update) | async-done | bytes 884752
  408.4 12.4 %all_gather.60 = bf16[3,144,1024]{2,0,1:T(4,128)(2,1)S(1)} all-gather(bf16[3,36,1024]{2,0,1:T(4,128)(2,1)S(1)} %copy.375), channel_id=1, replica_groups=mesh['rows'=32,'seq'=4] {'seq'}, dimensions={1}, use_global_device_ids=true | all-gather | bytes 1105920 | tf_op jit(solution)/shard_map/all_gather | solution.py:278
  427.7 9.0 reduce-scatter.21.cloned.1.call-done
  438.3 9.3 all_gather.52
  454.0 29.3 %all-reduce.28.cloned.1.call-done = bf16[3,144,1024]{2,1,0:T(8,128)(2,1)} async-done(((bf16[3,144,1024]{2,1,0:T(8,128)(2,1)}), bf16[3,144,1024]{2,1,0:T(8,128)(2,1)}) %all-reduce.28.cloned.1.call-update) | async-done | bytes 884752
  487.3 13.0 %all_gather.61 = bf16[3,144,1024]{2,0,1:T(4,128)(2,1)} all-gather(bf16[3,36,1024]{2,0,1:T(4,128)(2,1)S(1)} %copy.377), channel_id=1, replica_groups=mesh['rows'=32,'seq'=4] {'seq'}, dimensions={1}, use_global_device_ids=true | all-gather | bytes 1105920 | tf_op jit(solution)/shard_map/all_gather | solution.py:278
  539.5 12.7 %all_gather.56 = bf16[3,128,768]{2,1,0:T(8,128)(2,1)S(1)} all-gather(bf16[3,32,768]{2,1,0:T(8,128)(2,1)S(1)} %get-tuple-element.263), channel_id=1, replica_groups=mesh['rows'=32,'seq'=4] {'seq'}, dimensions={1}, use_global_device_ids=true | all-gather | bytes 737280 | tf_op jit(solution)/shard_map/all_gather | solution.py:277
  565.4 13.4 %all-reduce.30.cloned.1.call-done = bf16[3,144,1024]{2,1,0:T(8,128)(2,1)} async-done(((bf16[3,144,1024]{2,1,0:T(8,128)(2,1)}), bf16[3,144,1024]{2,1,0:T(8,128)(2,1)}) %all-reduce.30.cloned.1.call-update) | async-done | bytes 884752
  582.8 12.4 %all_gather.62 = bf16[3,144,1024]{2,0,1:T(4,128)(2,1)S(1)} all-gather(bf16[3,36,1024]{2,0,1:T(4,128)(2,1)S(1)} %copy.392), channel_id=1, replica_groups=mesh['rows'=32,'seq'=4] {'seq'}, dimensions={1}, use_global_device_ids=true | all-gather | bytes 1105920 | tf_op jit(solution)/shard_map/all_gather | solution.py:278
  613.6 9.6 all_gather.57
  644.7 6.6 concatenate.71.refs_2_
  660.0 12.4 %all_gather.63 = bf16[3,144,1024]{2,0,1:T(4,128)(2,1)S(1)} all-gather(bf16[3,36,1024]{2,0,1:T(4,128)(2,1)S(1)} %copy.394), channel_id=1, replica_groups=mesh['rows'=32,'seq'=4] {'seq'}, dimensions={1}, use_global_device_ids=true | all-gather | bytes 1105920 | tf_op jit(solution)/shard_map/all_gather | solution.py:278
  679.1 6.1 convert_reduce_fusion.12
  689.1 9.3 all_gather.58
  720.8 11.9 %reduce-scatter.29.cloned.1.call-done = bf16[3,32,768]{2,1,0:T(8,128)(2,1)} async-done(((bf16[3,128,768]{2,1,0:T(8,128)(2,1)}), bf16[3,32,768]{2,1,0:T(8,128)(2,1)}) %reduce-scatter.29.cloned.1.call-update) | async-done | bytes 147472 | tf_op jit(solution)/shard_map/reduce_scatter | solution.py:284
  735.6 9.3 all_gather.59
  781.7 91.2 %shard_map.638 = (f32[24,2560]{1,0:T(8,128)}, f32[32,1536]{1,0:T(8,128)}, f32[24,2304]{1,0:T(8,128)}, f32[32,1536]{1,0:T(8,128)}) custom-call(bf16[4,2,4,24,2560]{4,3,2,1,0:T(8,128)(2,1)} %pad_maximum_fusion.refs_0_, bf16[4,2,4,32,1536]{4,3,2,1,0:T(8,128)(2,1)} %pad_maximum_fusion.1.refs_1_, bf16[4,2,4,24,2304]{4,3,2,1,0:T(8,128)(2,1)} %concatenate.71.refs_2_, ...), custom_call_target="tpu_custom_call" | custom-call | tf_op jit(solution)/shard_map/pallas_call | solution.py:234
  881.4 126.3 %all-reduce.9 = (f32[2,256]{1,0:T(2,128)}, f32[1,768]{1,0:T(1,128)}, f32[2,256]{1,0:T(2,128)}, f32[1,256]{1,0:T(1,128)}, f32[2,192]{1,0:T(2,128)}, /*index=5*/f3...) all-reduce(f32[2,256]{1,0:T(2,128)S(1)} %pad_maximum_fusion.30, ...), channel_id=1, replica_groups=mesh['rows'=32,'seq'=4] {'rows'}, use_global_device_ids=true, to_apply=%region_74.75 | all-reduce | flops 3968 | bytes 31744 | tf_op jit(solution)/shard_map/psum | solution.py:781
  1014.8 159.5 %all-reduce.36.cloned.1.call-done = (f32[4,768]{1,0:T(4,128)}, f32[2,768]{1,0:T(2,128)}, f32[4,1024]{1,0:T(4,128)}, f32[2,1024]{1,0:T(2,128)}, f32[4,768]{1,0:T(...) async-done(((f32[4,768]{1,0:T(4,128)}, f32[2,768]{1,0:T(2,128)}, f32[4,1024]{1,0:T(4,128)}, f32[2,1024]{1,0:T(2,128)}, f32[4,768]{1,0:T(4,128)}, ...) | async-done | bytes 86032 | tf_op jit(solution)/shard_map/psum | solution.py:796
  (840 shorter events, 302.1 us)
Async XLA Ops:
  7.2 180.8 %all-reduce.20.cloned.1.call-start = ((), (), s32[]{:S(2)}) async-start(), calls=%async_computation.16 | async-start | bytes 1769472
  143.7 75.1 %reduce-scatter.17.cloned.1.call-start = ((), (), s32[]{:S(2)}) async-start(), calls=%async_computation.8 | async-start | bytes 737280 | tf_op jit(solution)/shard_map/reduce_scatter | solution.py:266
  148.6 116.8 %all-reduce.22.cloned.1.call-start = ((), (), s32[]{:S(2)}) async-start(), calls=%async_computation.17 | async-start | bytes 1769472
  151.4 430.4 %copy-start.92 = (f32[1,1024]{1,0:T(1,128)}, f32[1,1024]{1,0:T(1,128)S(1)}, u32[]{:S(2)}) copy-start(f32[1,1024]{1,0:T(1,128)S(1)} %get-tuple-element.325) | copy-start | bytes 12292
  154.6 152.1 %copy-start.40 = (bf16[768,576]{0,1:T(8,128)(2,1)}, bf16[768,576]{0,1:T(8,128)(2,1)S(1)}, u32[]{:S(2)}) copy-start(bf16[768,576]{0,1:T(8,128)(2,1)S(1)} %copy.346) | copy-start | bytes 2654212
  161.4 136.1 %copy-start.122 = (f32[768]{0:T(1024)}, f32[768]{0:T(1024)S(1)}, u32[]{:S(2)}) copy-start(f32[768]{0:T(1024)S(1)} %get-tuple-element.232) | copy-start | bytes 9220
  161.4 275.3 %copy-start.96 = (f32[768]{0:T(1024)}, f32[768]{0:T(1024)S(1)}, u32[]{:S(2)}) copy-start(f32[768]{0:T(1024)S(1)} %get-tuple-element.375) | copy-start | bytes 9220
  209.2 86.9 %reduce-scatter.19.cloned.1.call-start = ((), (), s32[]{:S(2)}) async-start(), calls=%async_computation.9 | async-start | bytes 737280 | tf_op jit(solution)/shard_map/reduce_scatter | solution.py:266
  237.3 105.2 %all-reduce.24.cloned.1.call-start = ((), (), s32[]{:S(2)}) async-start(), calls=%async_computation.18 | async-start | bytes 1769472
  266.8 315.0 %copy-start.106 = (f32[3,36]{1,0:T(4,128)}, f32[3,36]{1,0:T(4,128)S(1)}, u32[]{:S(2)}) copy-start(f32[3,36]{1,0:T(4,128)S(1)} %broadcast_multiply_fusion.2) | copy-start | bytes 1300
  267.0 314.8 %copy-start.117 = (f32[3,36]{1,0:T(4,128)}, f32[3,36]{1,0:T(4,128)S(1)}, u32[]{:S(2)}) copy-start(f32[3,36]{1,0:T(4,128)S(1)} %fusion.237) | copy-start | bytes 1300
  286.3 119.6 %all-reduce.26.cloned.1.call-start = ((), (), s32[]{:S(2)}) async-start(), calls=%async_computation.19 | async-start | bytes 1769472
  297.3 139.4 %copy-start.104 = (f32[3,32]{1,0:T(4,128)}, f32[3,32]{1,0:T(4,128)S(1)}, u32[]{:S(2)}) copy-start(f32[3,32]{1,0:T(4,128)S(1)} %broadcast_multiply_fusion.6) | copy-start | bytes 1156
  297.5 139.2 %copy-start.114 = (f32[3,32]{1,0:T(4,128)}, f32[3,32]{1,0:T(4,128)S(1)}, u32[]{:S(2)}) copy-start(f32[3,32]{1,0:T(4,128)S(1)} %fusion.233) | copy-start | bytes 1156
  362.2 74.5 %reduce-scatter.21.cloned.1.call-start = ((), (), s32[]{:S(2)}) async-start(), calls=%async_computation.10 | async-start | bytes 737280 | tf_op jit(solution)/shard_map/reduce_scatter | solution.py:266
  366.0 117.3 %all-reduce.28.cloned.1.call-start = ((), (), s32[]{:S(2)}) async-start(), calls=%async_computation.20 | async-start | bytes 1769472
  437.9 175.0 %copy-start.108 = (f32[3,32]{1,0:T(4,128)}, f32[3,32]{1,0:T(4,128)S(1)}, u32[]{:S(2)}) copy-start(f32[3,32]{1,0:T(4,128)S(1)} %broadcast_multiply_fusion.5) | copy-start | bytes 1156
  438.1 174.8 %copy-start.119 = (f32[3,32]{1,0:T(4,128)}, f32[3,32]{1,0:T(4,128)S(1)}, u32[]{:S(2)}) copy-start(f32[3,32]{1,0:T(4,128)S(1)} %fusion.234) | copy-start | bytes 1156
  438.1 99.4 %reduce-scatter.23.cloned.1.call-start = ((), (), s32[]{:S(2)}) async-start(), calls=%async_computation.11 | async-start | bytes 737280 | tf_op jit(solution)/shard_map/reduce_scatter | solution.py:266
  453.9 124.9 %all-reduce.30.cloned.1.call-start = ((), (), s32[]{:S(2)}) async-start(), calls=%async_computation.21 | async-start | bytes 1769472
  532.2 77.3 %reduce-scatter.25.cloned.1.call-start = ((), (), s32[]{:S(2)}) async-start(), calls=%async_computation.12 | async-start | bytes 737280 | tf_op jit(solution)/shard_map/reduce_scatter | solution.py:284
  565.3 90.8 %all-reduce.32.cloned.1.call-start = ((), (), s32[]{:S(2)}) async-start(), calls=%async_computation.22 | async-start | bytes 1769472
  605.0 81.8 %reduce-scatter.27.cloned.1.call-start = ((), (), s32[]{:S(2)}) async-start(), calls=%async_computation.13 | async-start | bytes 737280 | tf_op jit(solution)/shard_map/reduce_scatter | solution.py:284
  643.9 88.8 %reduce-scatter.29.cloned.1.call-start = ((), (), s32[]{:S(2)}) async-start(), calls=%async_computation.14 | async-start | bytes 737280 | tf_op jit(solution)/shard_map/reduce_scatter | solution.py:284
  704.7 306.2 %all-reduce.34.cloned.1.call-start = ((), (), s32[]{:S(2)}) async-start(), calls=%async_computation.23 | async-start | bytes 1769472
  754.1 259.0 %reduce-scatter.31.cloned.1.call-start = ((), (), s32[]{:S(2)}) async-start(), calls=%async_computation.15 | async-start | bytes 737280 | tf_op jit(solution)/shard_map/reduce_scatter | solution.py:284
  776.3 398.1 %all-reduce.36.cloned.1.call-start = ((), (), s32[]{:S(2)}) async-start(), calls=%async_computation.24 | async-start | bytes 172032 | tf_op jit(solution)/shard_map/psum | solution.py:796
  873.0 135.3 %copy-start.195 = (f32[1,768]{1,0:T(1,128)S(1)}, f32[1,768]{1,0:T(1,128)}, u32[]{:S(2)}) copy-start(f32[1,768]{1,0:T(1,128)} %stack.182) | copy-start | bytes 9220
  873.0 135.3 %copy-start.196 = (f32[1,768]{1,0:T(1,128)S(1)}, f32[1,768]{1,0:T(1,128)}, u32[]{:S(2)}) copy-start(f32[1,768]{1,0:T(1,128)} %stack.180) | copy-start | bytes 9220
  873.1 137.1 %copy-start.70 = (f32[24,2304]{1,0:T(8,128)S(1)}, f32[24,2304]{1,0:T(8,128)}, u32[]{:S(2)}) copy-start(f32[24,2304]{1,0:T(8,128)} %get-tuple-element.50) | copy-start | bytes 663556
  876.2 134.7 %copy-start.131 = (f32[3,36]{1,0:T(4,128)S(1)}, f32[3,36]{1,0:T(4,128)}, u32[]{:S(2)}) copy-start(f32[3,36]{1,0:T(4,128)} %copy-done.130) | copy-start | bytes 1300
  876.2 134.7 %copy-start.145 = (f32[3,36]{1,0:T(4,128)S(1)}, f32[3,36]{1,0:T(4,128)}, u32[]{:S(2)}) copy-start(f32[3,36]{1,0:T(4,128)} %copy-done.144) | copy-start | bytes 1300
  (231 other events, 3156.4 us)
Sparse Core Ops, SparseCore 0:
  143.8 44.1 all-reduce.19
  190.6 28.1 reduce-scatter.16
  221.3 44.0 all-reduce.21
  267.9 28.1 reduce-scatter.18
  298.4 44.0 all-reduce.23
  362.3 43.5 all-reduce.25
  408.5 28.1 reduce-scatter.20
  439.2 44.0 all-reduce.27
  485.9 28.1 reduce-scatter.22
  532.3 46.3 all-reduce.29
  581.4 28.1 reduce-scatter.24
  611.9 44.1 all-reduce.31
  658.7 28.0 reduce-scatter.26
  704.9 27.8 reduce-scatter.28
  754.2 43.5 all-reduce.33
  800.2 28.1 reduce-scatter.30
  1011.0 163.2 all-reduce.35

commit v2 on v1

v2 whole, which is shorter than its diff:
```python
import jax
import jax.numpy as jnp
from jax import lax
from jax.experimental import pallas as pl
from jax.experimental.pallas import tpu as pltpu
from jax.sharding import PartitionSpec as P

MESH = pl.DeviceIdType.MESH
VMEM = pltpu.VMEM
DMA = pltpu.SemaphoreType.DMA


class Place:
    def __init__(self):
        r = lax.axis_index("rows")
        s = lax.axis_index("seq")
        self.r, self.s = r, s
        self.x, self.z, self.y = r // 8, (r // 4) % 2, r % 4
        self.zh, self.c = s // 2, s % 2

    def dev(self, x, z, y):
        return ((x * 2 + z) * 4 + y, self.s)

    def along(self, axis, step):
        x, z, y = self.x, self.z, self.y
        if axis == "x":
            return self.dev((x + step) % 4, z, y)
        if axis == "y":
            return self.dev(x, z, (y + step) % 4)
        return self.dev(x, 1 - z, y)


def greet(devices):
    barrier = pltpu.get_barrier_semaphore()
    for device in devices:
        pl.semaphore_signal(barrier, inc=1, device_id=device, device_id_type=MESH)
    pl.semaphore_wait(barrier, len(devices))


def push(src, dst, sems, k, device):
    copy = pltpu.make_async_remote_copy(
        src_ref=src, dst_ref=dst, send_sem=sems.at[0, k], recv_sem=sems.at[1, k],
        device_id=device, device_id_type=MESH)
    copy.start()
    return copy


def gather_steps(me, own, buf, sems, order):
    x, z, y = me.x, me.z, me.y
    sent = []
    first = push(own, buf.at[x, z, y], sems, 0, me.along("z", 1))
    local = pltpu.make_async_copy(own, buf.at[x, z, y], sems.at[0, 9])
    local.start()
    yield
    local.wait()
    first.wait()
    k = 1
    for stage, axis in enumerate(order):
        if axis == "x":
            def view(step, half):
                at = (x + step) % 4
                if stage == 0:
                    return buf.at[at, :, y] if half is None else buf.at[at, half, y]
                return buf.at[at] if half is None else buf.at[at, :, pl.ds(2 * half, 2)]
        else:
            def view(step, half):
                at = (y + step) % 4
                if stage == 0:
                    return buf.at[x, :, at] if half is None else buf.at[x, half, at]
                return buf.at[:, :, at] if half is None else buf.at[pl.ds(2 * half, 2), :, at]
        right, left = me.along(axis, 1), me.along(axis, 3)
        to_right = push(view(0, None), view(0, None), sems, k, right)
        to_left = push(view(0, None), view(0, None), sems, k + 1, left)
        yield
        to_right.wait_recv()
        on_right = push(view(3, 0), view(3, 0), sems, k + 2, right)
        to_left.wait_recv()
        on_left = push(view(1, 1), view(1, 1), sems, k + 3, left)
        yield
        on_right.wait_recv()
        on_left.wait_recv()
        sent += [to_right, to_left, on_right, on_left]
        k += 4
    for copy in sent:
        copy.wait_send()


def run_together(steps):
    steps = list(steps)
    while steps:
        alive = []
        for step in steps:
            try:
                next(step)
                alive.append(step)
            except StopIteration:
                pass
        steps = alive


class Bag:
    pass


def call(kernel, inputs, outs, scratch, collective_id=None, hbm=()):
    names = list(inputs) + list(outs) + list(scratch)

    def body(*refs):
        bag = Bag()
        for name, ref in zip(names, refs):
            setattr(bag, name, ref)
        kernel(bag)

    def space(name):
        return pl.BlockSpec(memory_space=pl.ANY if name in hbm else pltpu.VMEM)
    results = pl.pallas_call(
        body, out_shape=list(outs.values()), in_specs=[space(n) for n in inputs], out_specs=[space(n) for n in outs],
        scratch_shapes=list(scratch.values()),
        compiler_params=pltpu.CompilerParams(collective_id=collective_id, has_side_effects=collective_id is not None,
                                             vmem_limit_bytes=63 * 1024 * 1024),
    )(*inputs.values())
    return dict(zip(outs, results))


class Trade:
    def __init__(self, me, pairs, sems):
        self.me, self.pairs, self.sems = me, pairs, sems

    def copies(self):
        return [pltpu.make_async_remote_copy(
            src_ref=src, dst_ref=dst, send_sem=self.sems.at[0, k], recv_sem=self.sems.at[1, k],
            device_id=self.me.along("z", 1), device_id_type=MESH) for k, (src, dst) in enumerate(self.pairs)]

    def start(self):
        @pl.when(self.me.zh == 1)
        def _():
            for copy in self.copies():
                copy.start()

        @pl.when(self.me.zh == 0)
        def _():
            for src, dst in self.pairs:
                dst[...] = src[...]

    def finish(self):
        @pl.when(self.me.zh == 1)
        def _():
            for copy in self.copies():
                copy.wait()


def near(me):
    return [me.along("z", 1), me.along("x", 1), me.along("x", 3), me.along("y", 1), me.along("y", 3)]


def front_kernel(g):
    me = Place()
    names = [f"{b}{i}" for b in range(2) for i in range(2)]
    for name in names:
        pack, proj = getattr(g, "pack" + name), getattr(g, "proj" + name)
        a = proj.shape[2]
        for c in range(3):
            pack[:, c * a:(c + 1) * a] = proj[c]
        at = 3 * a
        for part in ("out", "up", "down"):
            ref = getattr(g, part + name)
            pack[:, at:at + ref.shape[1]] = ref[...]
            at += ref.shape[1]
    greet(near(me))
    trade = Trade(me, [(g.x0, g.x0_got), (g.x1, g.x1_got), (g.lengths0, g.lengths0_got), (g.lengths1, g.lengths1_got),
                       (g.cot0, g.cot0_got), (g.cot1, g.cot1_got)], g.trade_sems)
    trade.start()
    run_together(gather_steps(me, getattr(g, "pack" + n), getattr(g, "whole" + n), getattr(g, "sems" + n),
                              "yx" if n[1] == "1" else "xy") for n in names)
    trade.finish()
    for name in ("x0", "x1", "cot0", "cot1", "lengths0", "lengths1"):
        getattr(g, name + "_out")[...] = getattr(g, name + "_got")[...]


def front(inputs):
    outs, scratch, hbm = {}, {}, []
    for b in range(2):
        for i in range(2):
            n = f"{b}{i}"
            rows = inputs["up" + n].shape[0]
            cols = 3 * inputs["proj" + n].shape[2] + sum(inputs[p + n].shape[1] for p in ("out", "up", "down"))
            scratch["pack" + n] = VMEM((rows, cols), jnp.bfloat16)
            scratch["sems" + n] = DMA((2, 10))
            outs["whole" + n] = jax.ShapeDtypeStruct((4, 2, 4, rows, cols), jnp.bfloat16)
            hbm.append("whole" + n)
    for name in ("x0", "x1", "cot0", "cot1", "lengths0", "lengths1"):
        scratch[name + "_got"] = VMEM(inputs[name].shape, inputs[name].dtype)
        outs[name + "_out"] = jax.ShapeDtypeStruct(inputs[name].shape, inputs[name].dtype)
    scratch["trade_sems"] = DMA((2, 6))
    return call(front_kernel, inputs, outs, scratch, 0, hbm)


def add_slabs(me, dst, src, count):
    def one(i, carry):
        at = dst(i)
        at[...] = (at[...].astype(jnp.float32) + src(i)[...].astype(jnp.float32)).astype(at.dtype)
        return carry
    lax.fori_loop(0, count, one, 0)


def reduce_steps(me, buf, out, halves, chunks, small_halves, small_chunks, last, sems, order):
    x, z, y = me.x, me.z, me.y
    sent = []
    k = 0
    for stage, axis in enumerate(order):
        half_in, chunk_in = (halves, chunks) if stage == 0 else (small_halves, small_chunks)
        place = x if axis == "x" else y
        if axis == "x":
            def view(step, half=None):
                at = (x + step) % 4
                if stage == 0:
                    return buf.at[at] if half is None else buf.at[at, :, pl.ds(2 * half, 2)]
                return buf.at[at, :, y] if half is None else buf.at[at, half, y]
        else:
            def view(step, half=None):
                at = (y + step) % 4
                if stage == 0:
                    return buf.at[:, :, at] if half is None else buf.at[pl.ds(2 * half, 2), :, at]
                return buf.at[x, :, at] if half is None else buf.at[x, half, at]
        right, left = me.along(axis, 1), me.along(axis, 3)
        a = push(view(2, 0), half_in.at[0], sems, k, right)
        b = push(view(2, 1), half_in.at[1], sems, k + 1, left)
        yield
        if stage == 0:
            def half_slab(step, half):
                at = (place + step) % 4
                if axis == "x":
                    return lambda i: buf.at[at, i // 2, 2 * half + i % 2]
                return lambda i: buf.at[2 * half + i // 2, i % 2, at]

            def full_slab(i):
                return buf.at[x, i // 4, i % 4] if axis == "x" else buf.at[i // 2, i % 2, y]
            n_half, n_full = 4, 8
        else:
            def half_slab(step, half):
                at = (place + step) % 4
                return lambda i: buf.at[at, half, y] if axis == "x" else buf.at[x, half, at]

            def full_slab(i):
                return buf.at[x, i, y]
            n_half, n_full = 1, 2

        def in_slab(ref, d):
            if stage == 1:
                return (lambda i: ref.at[d]) if ref is half_in else (lambda i: ref.at[d, i])
            wide = ref.shape[2]
            return lambda i: ref.at[d, i // wide, i % wide]
        a.wait_recv()
        add_slabs(me, half_slab(1, 0), in_slab(half_in, 0), n_half)
        c = push(view(1), chunk_in.at[0], sems, k + 2, right)
        b.wait_recv()
        add_slabs(me, half_slab(3, 1), in_slab(half_in, 1), n_half)
        d = push(view(3), chunk_in.at[1], sems, k + 3, left)
        yield
        c.wait_recv()
        add_slabs(me, full_slab, in_slab(chunk_in, 0), n_full)
        d.wait_recv()
        add_slabs(me, full_slab, in_slab(chunk_in, 1), n_full)
        sent += [a, b, c, d]
        k += 4
    e = push(buf.at[x, 1 - z, y], last, sems, k, me.along("z", 1))
    yield
    e.wait_recv()
    out[...] = buf[x, z, y].astype(jnp.float32) + last[...].astype(jnp.float32)
    sent.append(e)
    for copy in sent:
        copy.wait_send()


def reduce_scratch(order, rows, cols):
    lead = (2, 4) if order[0] == "x" else (4, 2)
    bf = jnp.bfloat16
    return [VMEM((2, 2, 2, rows, cols), bf), VMEM((2,) + lead + (rows, cols), bf),
            VMEM((2, rows, cols), bf), VMEM((2, 2, rows, cols), bf), VMEM((rows, cols), bf), DMA((2, 9))]


def total_steps(me, team, vecs, cols, got, slots, small, vec_out, col_out, sems):
    wide = vecs.shape[1] // 4

    def quarter(k):
        return pl.ds(pl.multiple_of(k * wide, 128), wide)
    mates = ((team.sib, team.sib_slab), (team.mate, team.mate_slab), (team.far, team.far_slab))
    sent = [push(vecs.at[:, quarter(slab)], got.at[k], sems, k, device) for k, (device, slab) in enumerate(mates)]
    yield
    for copy in sent:
        copy.wait_recv()
    small[:, :wide] = vecs[:, quarter(team.own)] + got[0] + got[1] + got[2]
    small[:, wide:] = cols[...]
    k = 3
    for stage, (axis, place, count) in enumerate((("x", me.x, 4), ("y", me.y, 4), ("z", me.z, 2))):
        slots[stage, place] = small[...]
        copies = [push(slots.at[stage, place], slots.at[stage, place], sems, k + n, me.along(axis, n + 1))
                  for n in range(count - 1)]
        k += count - 1
        yield
        for copy in copies:
            copy.wait_recv()
        total = slots[stage, 0] + slots[stage, 1]
        if count == 4:
            total = total + slots[stage, 2] + slots[stage, 3]
        small[...] = total
        sent += copies
    col_out[...] = small[:, wide:]
    vec_out[:, quarter(team.own)] = small[:, :wide]
    last = [push(vec_out.at[:, quarter(team.own)], vec_out.at[:, quarter(team.own)], sems, k + n, device)
            for n, (device, slab) in enumerate(mates)]
    yield
    for copy in last:
        copy.wait_recv()
    for copy in sent + last:
        copy.wait_send()


def back_kernel(g):
    me = Place()
    team = Team(me)
    names = [f"{b}{i}" for b in range(2) for i in range(2)]
    loads = []
    for k, n in enumerate(names):
        loads.append(pltpu.make_async_copy(getattr(g, "dw" + n), getattr(g, "held" + n), g.load_sems.at[k]))
        loads[-1].start()
    greet(near(me) + [me.along("x", 2), me.along("y", 2), team.sib, team.mate, team.far])
    trade = Trade(me, [(g.out0, g.out0_got), (g.out1, g.out1_got), (g.grad0, g.grad0_got), (g.grad1, g.grad1_got)],
                  g.trade_sems)
    trade.start()
    for copy in loads:
        copy.wait()
    steps = []
    for n in names:
        steps.append(reduce_steps(me, getattr(g, "held" + n), getattr(g, "sum" + n),
                                  *[getattr(g, f"scratch{n}_{k}") for k in range(6)], "xy" if n[1] == "1" else "yx"))
    steps.append(total_steps(me, team, g.vecs, g.cols, g.vec_got, g.slots, g.small, g.vec_sum, g.cols_sum, g.total_sems))
    run_together(steps)
    trade.finish()
    g.vecs_out[...] = g.vec_sum[...]
    for name in ("out0", "out1", "grad0", "grad1"):
        getattr(g, name + "_done")[...] = getattr(g, name + "_got")[...]


def back(inputs):
    outs, scratch, hbm = {}, {}, []
    for b in range(2):
        for i in range(2):
            n = f"{b}{i}"
            shape = inputs["dw" + n].shape
            hbm.append("dw" + n)
            scratch["held" + n] = VMEM(shape, jnp.bfloat16)
            for k, s in enumerate(reduce_scratch("xy" if i else "yx", shape[3], shape[4])):
                scratch[f"scratch{n}_{k}"] = s
            outs["sum" + n] = jax.ShapeDtypeStruct(shape[3:], jnp.float32)
    vec, col = inputs["vecs"].shape, inputs["cols"].shape
    f32 = jnp.float32
    scratch["vec_got"] = VMEM((3, 8, vec[1] // 4), f32)
    scratch["small"] = VMEM((8, vec[1] // 4 + col[1]), f32)
    scratch["slots"] = VMEM((3, 4, 8, vec[1] // 4 + col[1]), f32)
    scratch["vec_sum"] = VMEM(vec, f32)
    scratch["load_sems"] = DMA((4,))
    scratch["trade_sems"] = DMA((2, 4))
    scratch["total_sems"] = DMA((2, 13))
    outs["vecs_out"] = jax.ShapeDtypeStruct(vec, f32)
    outs["cols_sum"] = jax.ShapeDtypeStruct(col, f32)
    for name in ("out0", "out1", "grad0", "grad1"):
        scratch[name + "_got"] = VMEM(inputs[name].shape, inputs[name].dtype)
        outs[name + "_done"] = jax.ShapeDtypeStruct(inputs[name].shape, inputs[name].dtype)
    return call(back_kernel, inputs, outs, scratch, 1, hbm)


def finish_kernel(g):
    for i, count in enumerate((32, 36)):
        for name in ("out", "grad"):
            src, dst = getattr(g, f"{name}{i}"), getattr(g, f"{name}{i}_done")
            if i == 0:
                dst[...] = src[...].reshape(dst.shape)
            else:
                whole = src[...].astype(jnp.float32)
                for b in range(3):
                    dst[b] = whole[b * count:(b + 1) * count].astype(dst.dtype)
    at = 0
    for k, n in enumerate(f"{b}{i}" for b in range(2) for i in range(2)):
        total = getattr(g, "sum" + n)
        proj, out, up, down = [getattr(g, p + n) for p in ("proj", "out", "up", "down")]
        a, f = proj.shape[2], up.shape[1]
        for c in range(3):
            proj[c] = total[:, c * a:(c + 1) * a]
        out[...] = total[:, 3 * a:4 * a]
        up[...] = total[:, 4 * a:4 * a + f]
        down[...] = total[:, 4 * a + f:]
        head_bias, up_bias, bias, gain = [getattr(g, p + n) for p in ("head_bias", "up_bias", "bias", "gain")]
        head_bias[0:1] = g.cols[2 * k:2 * k + 1, :a]
        head_bias[1:2] = g.cols[2 * k:2 * k + 1, 2 * a:3 * a]
        up_bias[...] = g.cols[2 * k + 1:2 * k + 2, :f]
        width = bias.shape[1]
        bias[...] = g.vecs[0:4, at:at + width]
        gain[...] = g.vecs[4:6, at:at + width]
        at += width


F32, BF16 = jnp.float32, jnp.bfloat16
NN, NT, TN = ((1,), (0,)), ((1,), (1,)), ((0,), (0,))
EPS = 1e-05
MASKED = -1000000000.0


class Shape:
    def __init__(self, part, width, inner, hidden, head):
        self.part, self.width, self.inner, self.hidden, self.head = part, width, inner, hidden, head
        self.tokens = 4 * part
        self.out_at = 3 * inner
        self.up_at = 4 * inner
        self.down_at = 4 * inner + hidden
        self.columns = 4 * inner + 2 * hidden


def dot(a, b, dims):
    return lax.dot_general(a, b, (dims, ((), ())), preferred_element_type=F32)


def loop(count, body):
    def step(i, carry):
        body(i)
        return carry
    lax.fori_loop(0, count, step, 0)


def lanes(i, size=256, base=0):
    return pl.ds(pl.multiple_of(base + i * size, 128), size)


def rows16(i):
    return pl.ds(pl.multiple_of(i * 16, 16), 16)


class Team:
    def __init__(self, me):
        self.me = me
        self.own = me.s
        self.sib_slab = me.zh * 2 + 1 - me.c
        self.mate_slab = (1 - me.zh) * 2 + me.c
        self.far_slab = (1 - me.zh) * 2 + 1 - me.c
        self.sib = (me.r, self.sib_slab)
        self.far = ((me.x * 2 + 1 - me.z) * 4 + me.y, self.far_slab)
        self.mate = ((me.x * 2 + 1 - me.z) * 4 + me.y, self.mate_slab)


class Wire:
    def __init__(self, team, part, from_sib, from_mate, sems):
        self.team, self.part, self.from_sib, self.from_mate, self.sems = team, part, from_sib, from_mate, sems

    def gather_start(self, buf):
        t = self.team
        self.buf = buf
        self.over = push(buf.at[t.own], buf.at[t.own], self.sems, 0, t.mate)
        self.beside = push(buf.at[t.own], buf.at[t.own], self.sems, 1, t.sib)

    def gather_mid(self):
        t = self.team
        self.over.wait_recv()
        self.on = push(self.buf.at[t.mate_slab], self.buf.at[t.mate_slab], self.sems, 2, t.sib)

    def gather_end(self):
        self.beside.wait_recv()
        self.on.wait_recv()
        for copy in (self.over, self.beside, self.on):
            copy.wait_send()

    def reduce_start(self):
        t = self.team
        self.a = push(self.part.at[t.far_slab], self.from_sib.at[0], self.sems, 3, t.sib)
        self.b = push(self.part.at[t.sib_slab], self.from_sib.at[1], self.sems, 4, t.sib)

    def reduce_mid(self):
        t = self.team
        self.a.wait_recv()
        part, from_sib = self.part, self.from_sib

        def add(i):
            rows = rows16(i)
            part[t.mate_slab, rows] = (part[t.mate_slab, rows].astype(F32) + from_sib[0, rows].astype(F32)).astype(BF16)
        loop(part.shape[1] // 16, add)
        self.d = push(part.at[t.mate_slab], self.from_mate, self.sems, 5, t.mate)

    def reduce_end(self):
        self.b.wait_recv()
        self.d.wait_recv()
        for copy in (self.a, self.b, self.d):
            copy.wait_send()

    def total(self, rows):
        return (self.part[self.team.own, rows].astype(F32) + self.from_sib[1, rows].astype(F32)
                + self.from_mate[rows].astype(F32))


def normal(value):
    centre = jnp.mean(value, axis=-1, keepdims=True)
    moved = value - centre
    scale = lax.rsqrt(jnp.mean(moved * moved, axis=-1, keepdims=True) + EPS)
    return moved * scale, scale


def flat(ref):
    value = ref[...]
    return value.reshape(value.shape[0] * value.shape[1], value.shape[2])


def project(sh, v):
    whole = flat(v.xf)
    if sh.inner % 256:
        v.qkv[...] = (dot(whole, v.w[:, :3 * sh.inner], NN) + v.offset[...]).astype(BF16)
    else:
        def one(i):
            at = lanes(i)
            v.qkv[:, at] = (dot(whole, v.w[:, at], NN) + v.offset[:, at]).astype(BF16)
        loop(3 * sh.inner // 256, one)


def probabilities(query, key, col_ids, row_ids, scale):
    raw = dot(query, key, NT)
    scores = jnp.where(col_ids == row_ids, raw * scale, MASKED)
    grown = jnp.exp(scores - jnp.max(scores, axis=-1, keepdims=True))
    return grown * (1.0 / jnp.sum(grown, axis=-1, keepdims=True))


def attend(sh, v, kv):
    h, a = sh.head, sh.inner
    row_ids = kv.ids_row[...]
    for n in range(a // h):
        key = kv.qkv[:, a + n * h:a + (n + 1) * h]
        value = kv.qkv[:, 2 * a + n * h:2 * a + (n + 1) * h]

        def one(i):
            rows = pl.ds(pl.multiple_of(i * sh.part, 16), sh.part)
            p = probabilities(v.qkv[rows, n * h:(n + 1) * h], key, v.ids_col[rows], row_ids, h ** -0.5)
            v.mixed[rows, n * h:(n + 1) * h] = dot(p.astype(BF16), value, NN).astype(BF16)
        loop(4, one)


def spread_out(sh, v, left, at, size):
    def one(i):
        rows = lanes(i)
        result = dot(left, v.w[rows, at:at + size], NT)
        v.wire.part[:, :, rows] = result.reshape(4, sh.part, 256).astype(BF16)
    loop(sh.width // 256, one)


def norm_forward(sh, v, base, sums, which, result, low):
    bias = v.bias[pl.ds(which, 1)].astype(F32)
    shift = v.bias[pl.ds(2 + which, 1)].astype(F32)
    gain = v.gain[pl.ds(which, 1)].astype(F32)

    def one(i):
        rows = rows16(i)
        value = base[rows] + v.wire.total(rows) + bias
        sums[rows] = value
        value = normal(value)[0] * gain + shift
        result[rows] = value
        low[rows] = value.astype(BF16)
    loop(sh.part // 16, one)


def feed(sh, v):
    whole = flat(v.nf)
    k = (2.0 / jnp.pi) ** 0.5

    def one(i):
        at = lanes(i)
        u = dot(whole, v.w[:, lanes(i, 256, sh.up_at)], NN) + v.up_bias[:, at].astype(F32)
        square = u * u
        t = jnp.tanh(k * u * (1.0 + 0.044715 * square))
        half = 0.5 * (1.0 + t)
        v.active[:, at] = (u * half).astype(BF16)
        v.slope[:, at] = half + 0.5 * u * (1.0 - t * t) * (k * (1.0 + 3 * 0.044715 * square))
    loop(sh.hidden // 256, one)
    spread_out(sh, v, v.active[...], sh.down_at, sh.hidden)


def norm_backward(sh, v, grad, sums, which, result, low, vec, bias_row):
    gain = v.gain[pl.ds(which, 1)].astype(F32)

    def fold(value):
        return value[:8] + value[8:]

    def one(i, carry):
        rows = rows16(i)
        g = grad(rows)
        n, scale = normal(sums[rows])
        gn = g * gain
        out = scale * (gn - jnp.mean(gn, axis=-1, keepdims=True) - n * jnp.mean(gn * n, axis=-1, keepdims=True))
        rounded = out.astype(BF16)
        result[rows] = out
        low[rows] = rounded
        return (carry[0] + fold(rounded.astype(F32)), carry[1] + fold(g), carry[2] + fold(g * n))
    zero = jnp.zeros((8, sh.width), F32)
    totals = lax.fori_loop(0, sh.part // 16, one, (zero, zero, zero))
    for at, total in zip((bias_row, 2 + which, 4 + which), totals):
        vec[pl.ds(at, 1)] = jnp.sum(total, axis=0, keepdims=True)


def weight_grad(sh, v, left, right, at):
    def one(i):
        cut = lanes(i)
        piece = left[:, :, cut].reshape(sh.tokens, 256)
        v.dw[cut, at:at + right.shape[1]] = dot(piece, right[...], TN).astype(BF16)
    loop(sh.width // 256, one)


def feed_back(sh, v):
    whole = flat(v.gs)

    def one(i):
        at = lanes(i)
        grad = dot(whole, v.w[:, lanes(i, 256, sh.down_at)], NN)
        gu = (grad * v.slope[:, at]).astype(BF16)
        v.gu[:, at] = gu
        v.col_up[:, at] = jnp.sum(gu.astype(F32), axis=0, keepdims=True)
    loop(sh.hidden // 256, one)
    spread_out(sh, v, v.gu[...], sh.up_at, sh.hidden)


def attend_back(sh, v, kv, p_ref, s_ref):
    h, a = sh.head, sh.inner
    width = kv.qkv.shape[0]
    row_ids = kv.ids_row[...]
    scale = h ** -0.5
    for n in range(a // h):
        q_at, k_at, v_at = [slice(c * a + n * h, c * a + (n + 1) * h) for c in range(3)]
        key, value = kv.qkv[:, k_at], kv.qkv[:, v_at]

        def one(i):
            rows = pl.ds(pl.multiple_of(i * sh.part, 16), sh.part)
            p = probabilities(v.qkv[rows, q_at], key, v.ids_col[rows], row_ids, scale)
            gp = dot(v.gm[rows, q_at], value, NT)
            gs = (p * (gp - jnp.sum(gp * p, axis=-1, keepdims=True)) * scale).astype(BF16)
            p_ref[rows, :width] = p.astype(BF16)
            s_ref[rows, :width] = gs
            v.gp[rows, q_at] = dot(gs, key, NN).astype(BF16)
        loop(4, one)
        kv.gp[:, k_at] = dot(s_ref[:sh.tokens, :width], v.qkv[:, q_at], TN).astype(BF16)
        kv.gp[:, v_at] = dot(p_ref[:sh.tokens, :width], v.gm[:, q_at], TN).astype(BF16)


def block_forward(shapes, views, crossing, base, result, low):
    for v in views:
        v.wire.gather_start(v.xf)
    for v in views:
        v.wire.gather_mid()
    for sh, v in zip(shapes, views):
        v.wire.gather_end()
        project(sh, v)
    for i, (sh, v) in enumerate(zip(shapes, views)):
        attend(sh, v, views[1 - i] if crossing else v)
        spread_out(sh, v, v.mixed[...], sh.out_at, sh.inner)
        v.wire.reduce_start()
        if i == 1:
            views[0].wire.reduce_mid()
    views[1].wire.reduce_mid()
    for i, (sh, v) in enumerate(zip(shapes, views)):
        v.wire.reduce_end()
        norm_forward(sh, v, base[i], v.first, 0, v.normed, v.nf.at[v.wire.team.own])
        v.wire.gather_start(v.nf)
    for i, (sh, v) in enumerate(zip(shapes, views)):
        v.wire.gather_mid()
        v.wire.gather_end()
        feed(sh, v)
        v.wire.reduce_start()
        if i == 1:
            views[0].wire.reduce_mid()
    views[1].wire.reduce_mid()
    for i, (sh, v) in enumerate(zip(shapes, views)):
        v.wire.reduce_end()
        norm_forward(sh, v, v.normed, v.second, 1, result[i], low[i])


def block_backward(shapes, views, crossing, grads, results, scratch):
    own = views[0].wire.team.own
    for i, (sh, v) in enumerate(zip(shapes, views)):
        norm_backward(sh, v, grads[i], v.second, 1, v.normed, v.gs.at[own], v.vec, 1)
        v.wire.gather_start(v.gs)
    for i, (sh, v) in enumerate(zip(shapes, views)):
        v.wire.gather_mid()
        v.wire.gather_end()
        feed_back(sh, v)
        v.wire.reduce_start()
        if i == 1:
            views[0].wire.reduce_mid()
    views[1].wire.reduce_mid()
    weight_grad(shapes[0], views[0], views[0].gs, views[0].active, shapes[0].down_at)
    for i, (sh, v) in enumerate(zip(shapes, views)):
        v.wire.reduce_end()
        norm_backward(sh, v, lambda rows, v=v: v.normed[rows] + v.wire.total(rows), v.first, 0, v.normed,
                      v.gb.at[own], v.vec, 0)
        v.wire.gather_start(v.gb)
    weight_grad(shapes[1], views[1], views[1].gs, views[1].active, shapes[1].down_at)
    for v in views:
        v.wire.gather_mid()
    weight_grad(shapes[0], views[0], views[0].nf, views[0].gu, shapes[0].up_at)
    weight_grad(shapes[1], views[1], views[1].nf, views[1].gu, shapes[1].up_at)
    for i, (sh, v) in enumerate(zip(shapes, views)):
        v.wire.gather_end()
        v.gm[...] = dot(flat(v.gb), v.w[:, sh.out_at:sh.out_at + sh.inner], NN).astype(BF16)
    for i, (sh, v) in enumerate(zip(shapes, views)):
        attend_back(sh, v, views[1 - i] if crossing else v, *scratch)
    for i, (sh, v) in enumerate(zip(shapes, views)):
        spread_out(sh, v, v.gp[...], 0, 3 * sh.inner)
        v.wire.reduce_start()
        if i == 1:
            views[0].wire.reduce_mid()
    views[1].wire.reduce_mid()
    for sh, v in zip(shapes, views):
        weight_grad(sh, v, v.gb, v.mixed, sh.out_at)
        weight_grad(sh, v, v.xf, v.gp, 0)
        v.col_proj[:, :3 * sh.inner] = jnp.sum(v.gp[...].astype(F32), axis=0, keepdims=True)
    for i, (sh, v) in enumerate(zip(shapes, views)):
        v.wire.reduce_end()

        def one(j):
            rows = rows16(j)
            results[i](rows, v.normed[rows] + v.wire.total(rows))
        loop(sh.part // 16, one)


SHAPES = ((Shape(96, 768, 256, 768, 128), Shape(112, 1024, 256, 256, 128)),
          (Shape(96, 768, 192, 768, 64), Shape(112, 1024, 256, 256, 128)))


def set_ids(ref, lengths, per_part, part, axis):
    token = lax.broadcasted_iota(jnp.int32, ref.shape, axis)

    def over(value, size, most):
        return sum((value >= k * size).astype(jnp.int32) for k in range(1, most))
    p = over(token, part, 4)
    within = token - part * p
    row = over(within, per_part, 4)
    position = p * per_part + within - per_part * row
    ids = jnp.full(ref.shape, -1, jnp.int32)
    for b in range(3):
        bound = jnp.zeros((1, 1), jnp.int32)
        seg = jnp.full(ref.shape, 4 * b, jnp.int32)
        for j in range(4):
            bound = bound + lengths[b:b + 1, j:j + 1]
            seg = seg + (position >= bound).astype(jnp.int32)
        ids = jnp.where(row == b, seg, ids)
    ref[...] = ids.astype(F32)


def middle_kernel(g):
    me = Place()
    team = Team(me)
    loads = []
    for b in range(2):
        for i in range(2):
            copy = pltpu.make_async_copy(getattr(g, f"w_in{b}{i}"), getattr(g, f"w{b}{i}"), g.load_sem.at[2 * b + i])
            copy.start()
            loads.append(copy)
    greet([team.sib, team.mate])
    wires = [Wire(team, getattr(g, f"part{i}"), getattr(g, f"from_sib{i}"), getattr(g, f"from_mate{i}"),
                  getattr(g, f"sems{i}")) for i in range(2)]
    views = []
    lane = 0
    for b in range(2):
        pair = []
        for i in range(2):
            v = Bag()
            v.wire = wires[i]
            for name in ("w", "head_bias", "up_bias", "bias", "gain", "offset", "xf", "qkv", "mixed", "nf", "slope",
                         "active", "first", "second", "dw", "gm", "gp"):
                setattr(v, name, getattr(g, f"{name}{b}{i}"))
            for name in ("ids_col", "ids_row", "normed", "gs", "gb", "gu"):
                setattr(v, name, getattr(g, f"{name}{i}"))
            sh = SHAPES[b][i]
            k = 2 * (2 * b + i)
            v.vec = g.vecs.at[:, lane:lane + sh.width]
            lane += sh.width
            v.col_proj = g.cols.at[k:k + 1]
            v.col_up = g.cols.at[k + 1:k + 2]
            a = sh.inner
            v.offset[:, :a] = v.head_bias[0:1].astype(F32)
            v.offset[:, a:2 * a] = jnp.zeros((1, a), F32)
            v.offset[:, 2 * a:] = v.head_bias[1:2].astype(F32)
            pair.append(v)
        views.append(pair)
    g.vecs[...] = jnp.zeros_like(g.vecs)
    g.cols[...] = jnp.zeros_like(g.cols)
    for i, per_part in enumerate((32, 36)):
        for axis, name in enumerate(("ids_col", "ids_row")):
            set_ids(getattr(g, f"{name}{i}"), getattr(g, f"lengths{i}"), per_part, SHAPES[0][i].part, axis)
    x_in = (g.x0, g.x1)
    base = (g.base0, g.base1)
    for i in range(2):
        def one(j, i=i):
            rows = rows16(j)
            views[0][i].xf[team.own, rows] = x_in[i][rows]
            base[i][rows] = x_in[i][rows].astype(F32)
        loop(SHAPES[0][i].part // 16, one)
    loads[0].wait()
    loads[1].wait()
    block_forward(SHAPES[0], views[0], True, base, base, [views[1][i].xf.at[team.own] for i in range(2)])
    loads[2].wait()
    loads[3].wait()
    block_forward(SHAPES[1], views[1], False, base, base, (g.out0, g.out1))
    cots = (g.cot0, g.cot1)
    scratch = (g.p_ref, g.s_ref)

    def keep(i):
        def put(rows, value):
            base[i][rows] = value
        return put

    def give(i):
        out = (g.grad0, g.grad1)[i]

        def put(rows, value):
            out[rows] = value.astype(BF16)
        return put
    block_backward(SHAPES[1], views[1], False, [lambda rows, i=i: cots[i][rows].astype(F32) for i in range(2)],
                   [keep(0), keep(1)], scratch)
    saves = []
    for i in range(2):
        saves.append(pltpu.make_async_copy(views[1][i].dw, getattr(g, f"dw_out1{i}"), g.load_sem.at[2 + i]))
        saves[-1].start()
    block_backward(SHAPES[0], views[0], True, [lambda rows, i=i: base[i][rows] for i in range(2)],
                   [give(0), give(1)], scratch)
    for i in range(2):
        saves.append(pltpu.make_async_copy(views[0][i].dw, getattr(g, f"dw_out0{i}"), g.load_sem.at[i]))
        saves[-1].start()
    for copy in saves:
        copy.wait()


def middle(inputs):
    outs, scratch, hbm = {}, {}, []
    for i in range(2):
        sh = SHAPES[0][i]
        outs[f"out{i}"] = jax.ShapeDtypeStruct((sh.part, sh.width), BF16)
        outs[f"grad{i}"] = jax.ShapeDtypeStruct((sh.part, sh.width), BF16)
        scratch[f"base{i}"] = VMEM((sh.part, sh.width), F32)
        scratch[f"normed{i}"] = VMEM((sh.part, sh.width), F32)
        for name in ("gs", "gb"):
            scratch[f"{name}{i}"] = VMEM((4, sh.part, sh.width), BF16)
        scratch[f"gu{i}"] = VMEM((sh.tokens, sh.hidden), BF16)
        scratch[f"part{i}"] = VMEM((4, sh.part, sh.width), BF16)
        scratch[f"from_sib{i}"] = VMEM((2, sh.part, sh.width), BF16)
        scratch[f"from_mate{i}"] = VMEM((sh.part, sh.width), BF16)
        scratch[f"sems{i}"] = DMA((2, 6))
        scratch[f"ids_col{i}"] = VMEM((sh.tokens, 1), F32)
        scratch[f"ids_row{i}"] = VMEM((1, sh.tokens), F32)
    scratch["p_ref"] = VMEM((448, 448), BF16)
    scratch["s_ref"] = VMEM((448, 448), BF16)
    scratch["load_sem"] = DMA((4,))
    outs["vecs"] = jax.ShapeDtypeStruct((8, 2 * (768 + 1024)), F32)
    outs["cols"] = jax.ShapeDtypeStruct((8, 768), F32)
    for b in range(2):
        for i in range(2):
            sh = SHAPES[b][i]
            outs[f"dw_out{b}{i}"] = jax.ShapeDtypeStruct((sh.width, sh.columns), BF16)
            hbm += [f"dw_out{b}{i}", f"w_in{b}{i}"]
            scratch[f"offset{b}{i}"] = VMEM((1, 3 * sh.inner), F32)
            for name, shape, kind in (
                    ("w", (sh.width, sh.columns), BF16), ("dw", (sh.width, sh.columns), BF16),
                    ("xf", (4, sh.part, sh.width), BF16), ("nf", (4, sh.part, sh.width), BF16),
                    ("qkv", (sh.tokens, 3 * sh.inner), BF16), ("gp", (sh.tokens, 3 * sh.inner), BF16),
                    ("mixed", (sh.tokens, sh.inner), BF16), ("gm", (sh.tokens, sh.inner), BF16),
                    ("slope", (sh.tokens, sh.hidden), F32),
                    ("active", (sh.tokens, sh.hidden), BF16), ("first", (sh.part, sh.width), F32),
                    ("second", (sh.part, sh.width), F32)):
                scratch[f"{name}{b}{i}"] = VMEM(shape, kind)
    return call(middle_kernel, inputs, outs, scratch, 2, hbm)


def on_device(*args):
    text_in, image_in, text_lengths, image_lengths, text_cot, image_cot = args[:6]
    matrix_names = ("proj", "out", "up", "down")
    small_names = ("head_bias", "up_bias", "bias", "gain")

    def rows_of(value):
        value = value.reshape(-1, value.shape[-1])
        return jnp.pad(value, ((0, -value.shape[0] % 16), (0, 0)))
    tensors = {}
    for b in range(2):
        for i in range(2):
            at = 6 + 16 * b + 8 * i
            for name, value in zip(matrix_names + small_names, args[at:at + 8]):
                tensors[f"{name}{b}{i}"] = value.transpose(1, 0, 2) if name == "proj" else value
    names = [f"{b}{i}" for b in range(2) for i in range(2)]
    first = {"x0": rows_of(text_in), "x1": rows_of(image_in), "cot0": rows_of(text_cot), "cot1": rows_of(image_cot),
             "lengths0": text_lengths, "lengths1": image_lengths}
    moved = list(first)
    for n in names:
        for p in matrix_names:
            first[p + n] = tensors[p + n]
    got = front(first)
    inputs = {name: got[name + "_out"] for name in moved}
    for n in names:
        whole = got["whole" + n]
        inputs["w_in" + n] = whole.reshape(-1, whole.shape[-1])
        for p in small_names:
            inputs[p + n] = tensors[p + n]
    done = middle(inputs)
    last = {name: done[name] for name in ("vecs", "cols", "out0", "out1", "grad0", "grad1")}
    for n in names:
        whole = done["dw_out" + n]
        last["dw" + n] = whole.reshape(4, 2, 4, whole.shape[0] // 32, whole.shape[1])
    sums = back(last)
    ends = {"vecs": sums["vecs_out"], "cols": sums["cols_sum"]}
    outs = {}
    for name, like in (("out0", text_in), ("out1", image_in), ("grad0", text_in), ("grad1", image_in)):
        ends[name] = sums[name + "_done"]
        outs[name + "_done"] = jax.ShapeDtypeStruct(like.shape, like.dtype)
    for n in names:
        ends["sum" + n] = sums["sum" + n]
        for p in matrix_names + small_names:
            outs[p + n] = jax.ShapeDtypeStruct(tensors[p + n].shape, jnp.float32)
    return tuple(value.transpose(1, 0, 2) if name.startswith("proj") else value
                 for name, value in call(finish_kernel, ends, outs, {}).items())


def solution(mesh):
    kinds = [P("rows", None, "seq"), P("rows", "seq"), P("rows", "seq"), P("rows", "seq"), P(None, "seq"),
             P(None, "seq"), P(), P()] * 4
    position = P("rows", "seq", None)
    return jax.shard_map(
        on_device, mesh=mesh,
        in_specs=tuple([position, position, P("rows", None), P("rows", None), position, position] + kinds),
        out_specs=tuple([position] * 4 + kinds), check_vma=False)
```

time: 1200 us -> 457 us (0.38)
  waiting for transfers between devices: 382 us -> 0 us
  blocking collectives: 307 us -> 0 us
  Pallas kernels: 180 us -> 452 us
  matrix products: 137 us -> 0 us
  local copies, waits for them, and re-layouts: 103 us -> 3.38 us
  other arithmetic: 63.1 us -> 0 us
  between operations: 17.9 us -> 0.87 us
    pallas_call x2 -> x4, Pallas kernels: 180 us -> 452 us  [call(): pl.pallas_call(body, out_shape=list(outs.values()), in_specs=[space(n) fo...]
    all_gather x16 -> x0, blocking collectives: 181 us -> none  [the longest x4 50.5 us: spread_tokens(): lax.all_gather(image_part, 'seq', axis=1, tiled=True)]
    unnamed x25 -> x0, waiting for transfers between devices: 177 us -> none
    psum x1 -> x0, waiting for transfers between devices: 160 us -> none  [on_device(): lax.psum((cross_vecs[0][0], cross_vecs[0][1], cross_vecs[1][0], cross_vec...]
    dot_general x72 -> x0, matrix products: 137 us -> none  [the longest x4 12 us: attend_back(): jnp.einsum('bhqk,bkhd->bqhd', grad_scores, key_heads, preferred_element_t...]
    psum x1 -> x0, blocking collectives: 126 us -> none  [on_device(): lax.psum((cross_cols[0][0], cross_cols[0][1], cross_cols[1][0], cross_col...]
    reduce_scatter x8 -> x0, waiting for transfers between devices: 45.2 us -> none  [the longest x4 28.2 us: tokens_from_partials(): lax.psum_scatter(text_part.astype(jnp.bfloat16), 'seq', scatter_dimension...]
    reduce_sum x46 -> x0, other arithmetic: 32.5 us -> none  [the longest x8 13.5 us: layer_norm(): (summed - centre) * lax.rsqrt(spread + epsilon) * gain_vec + shift_vec]
  transfers between devices with their start and end apart: 17 -> 0, of which waited for: 14 -> 0; matrix products, arithmetic and copies ran while one was open for 20% -> 0% of each run, Pallas kernels for 8% -> 0%
where the time goes in v2:
time: 457 us; the launch traced here: 456 us
  Pallas kernels  452 us (99%)
    pallas_call x4, Pallas kernels, call(): pl.pallas_call(body, out_shape=list(outs.values()), in_specs=[space(n) fo...  452 us

profile of v2, /device:TPU:1, one launch (start us, length us, event | category | flops | bytes accessed | tf_op | source)
XLA Modules:
  0.0 456.3 jit_solution(15702529311157047668)
XLA Ops:
  0.7 1.0 reshape.109
  1.7 0.7 pad.7.refs_1_
  2.4 1.0 reshape.111
  3.4 0.7 pad.8.refs_3_
  4.1 89.0 %shard_map.637 = (bf16[4,2,4,24,2560]{4,3,2,1,0:T(8,128)(2,1)}, bf16[4,2,4,32,1536]{4,3,2,1,0:T(8,128)(2,1)}, bf16[4,2,4,24,2304]{4,3,2,1,0:T(8,128)(2,1)}, bf16...) custom-call(bf16[96,768]{1,0:T(8,128)(2,1)} %bitcast.26, ...), custom_call_target="tpu_custom_call" | custom-call | tf_op jit(solution)/shard_map/pallas_call | solution.py:116
  93.1 270.1 %shard_map.638 = (bf16[96,768]{1,0:T(8,128)(2,1)}, bf16[96,768]{1,0:T(8,128)(2,1)}, bf16[112,1024]{1,0:T(8,128)(2,1)}, bf16[112,1024]{1,0:T(8,128)(2,1)}, f32[8,...) custom-call(bf16[96,768]{1,0:T(8,128)(2,1)} %get-tuple-element.102.r, ...), custom_call_target="tpu_custom_call" | custom-call | tf_op jit(solution)/shard_map/pallas_call | solution.py:116
  363.2 90.1 %shard_map.639 = (f32[24,2560]{1,0:T(8,128)}, f32[32,1536]{1,0:T(8,128)}, f32[24,2304]{1,0:T(8,128)}, f32[32,1536]{1,0:T(8,128)}, f32[8,3584]{1,0:T(8,128)}, /*i...) custom-call(f32[8,3584]{1,0:T(8,128)} %get-tuple-element.112.refs_0_, ...), custom_call_target="tpu_custom_call" | custom-call | tf_op jit(solution)/shard_map/pallas_call | solution.py:116
  453.2 2.9 shard_map.640
